TPU v7x, 32 devices: a whole 2x2x4 slice. The times are simulated.
32 devices in a mesh: dp: 4 (over z), seq: 4 (over y, x), head: 2 (over core).
Axes of the slice: x: 2, y: 2, z: 4, core: 2. Of those that a mesh axis runs over, the one named last changes fastest.
Arguments:
- inputs: bfloat16 [32, 512, 768], P(('dp', 'head'), 'seq'), may hold values from -6 to 6
- dec_in: bfloat16 [8, 4, 768], P(('dp', 'head'), 'seq'), may hold values from -6 to 6
- cotangent: bfloat16 [8, 4, 768], P(('dp', 'head'), 'seq'), may hold values from -6 to 6
- lengths: int32 [32], P(('dp', 'head')), may hold values from 40 to 512, as said below
- bucket_table: int32 [1023], replicated, may hold values from 0 to 31, as said below
- square: float32 [10, 768, 768], P(None, ('dp', 'seq', 'head'))
- square_m: float32 [10, 768, 768], P(None, ('dp', 'seq', 'head')), may hold values from -0.0004272461 to 0.0004272461
- square_v: float32 [10, 768, 768], P(None, ('dp', 'seq', 'head')), may hold values from 6.5e-11 to 2.6e-10
- ffn_in: float32 [2, 768, 3072], P(None, ('dp', 'seq', 'head')), may hold values from -0.21875 to 0.21875
- ffn_in_m: float32 [2, 768, 3072], P(None, ('dp', 'seq', 'head')), may hold values from -0.0004272461 to 0.0004272461
- ffn_in_v: float32 [2, 768, 3072], P(None, ('dp', 'seq', 'head')), may hold values from 6.5e-11 to 2.6e-10
- ffn_out: float32 [2, 3072, 768], P(None, ('dp', 'seq', 'head')), may hold values from -0.109375 to 0.109375
- ffn_out_m: float32 [2, 3072, 768], P(None, ('dp', 'seq', 'head')), may hold values from -0.0004272461 to 0.0004272461
- ffn_out_v: float32 [2, 3072, 768], P(None, ('dp', 'seq', 'head')), may hold values from 6.5e-11 to 2.6e-10
- gains: float32 [6, 768], P(None, ('dp', 'seq', 'head'))
- gains_m: float32 [6, 768], P(None, ('dp', 'seq', 'head')), may hold values from -0.0004272461 to 0.0004272461
- gains_v: float32 [6, 768], P(None, ('dp', 'seq', 'head')), may hold values from 6.5e-11 to 2.6e-10
- rel_bias: float32 [32, 12], replicated, may hold values from -3 to 3
- rel_bias_m: float32 [32, 12], replicated, may hold values from -0.0004272461 to 0.0004272461
- rel_bias_v: float32 [32, 12], replicated, may hold values from 6.5e-11 to 2.6e-10
Outputs:
- dec_out: bfloat16 [8, 4, 768], P(('dp', 'head'), 'seq')
- input_grad: float32 [32, 512, 768], P(('dp', 'head'), 'seq')
- grad_norm: float32 [], replicated
- square_new: float32 [10, 768, 768], P(None, ('dp', 'seq', 'head'))
- square_m_new: float32 [10, 768, 768], P(None, ('dp', 'seq', 'head'))
- square_v_new: float32 [10, 768, 768], P(None, ('dp', 'seq', 'head'))
- ffn_in_new: float32 [2, 768, 3072], P(None, ('dp', 'seq', 'head'))
- ffn_in_m_new: float32 [2, 768, 3072], P(None, ('dp', 'seq', 'head'))
- ffn_in_v_new: float32 [2, 768, 3072], P(None, ('dp', 'seq', 'head'))
- ffn_out_new: float32 [2, 3072, 768], P(None, ('dp', 'seq', 'head'))
- ffn_out_m_new: float32 [2, 3072, 768], P(None, ('dp', 'seq', 'head'))
- ffn_out_v_new: float32 [2, 3072, 768], P(None, ('dp', 'seq', 'head'))
- gains_new: float32 [6, 768], P(None, ('dp', 'seq', 'head'))
- gains_m_new: float32 [6, 768], P(None, ('dp', 'seq', 'head'))
- gains_v_new: float32 [6, 768], P(None, ('dp', 'seq', 'head'))
- rel_bias_new: float32 [32, 12], replicated
- rel_bias_m_new: float32 [32, 12], replicated
- rel_bias_v_new: float32 [32, 12], replicated
Inputs may be any that keep to these rules, and one draw needn't show every extreme that they name: Row n holds one document in positions 0 to lengths[n] - 1, the rest is padding; in every group of 4 consecutive rows at least one row has length 512. `bucket_table`: entry j is the bucket of relative position j - 511; buckets of offsets of one sign do not fall as the distance grows; non-positive offsets use buckets below 16, positive ones the others.
All inputs are finite; a program needn't handle non-finite values.
Results may differ from a plain program's by a relative error of at most 0.02.
The roundings to bfloat16 on the way count: a program that leaves them out, or rounds other values in their place, can miss the bound.
Values may be sent and summed in bfloat16 or wider, within the bound.
A program may use at most 320 MiB of HBM per device.

v0:
```python
import math

import jax
import jax.numpy as jnp
from jax import lax
from jax.sharding import PartitionSpec as P

H = 12
HD = 64
STEP = 5


norm_eps = 1e-06
neg_fill = -1e30
beta_one = 0.9
beta_two = 0.999
adam_eps = 1e-08
decay_rate = 0.01
rate_matrix = 0.05
rate_small = 0.5
clip_bound = 1.0
highest_precision = lax.Precision.HIGHEST


def rms_gain(values_in, gain_row):
    return (
        values_in
        * lax.rsqrt(jnp.mean(values_in * values_in, axis=-1, keepdims=True) + norm_eps)
        * gain_row
    )


def gelu_tanh(values_in):
    return jax.nn.gelu(values_in, approximate=True)


def matmul(left, right):
    return jnp.dot(left, right, preferred_element_type=jnp.float32)


def token_outer(left, right):
    return jnp.einsum("rqd,rqe->de", left, right, preferred_element_type=jnp.float32)


def rms_pull(values_in, gain_row, incoming):
    _, pull = jax.vjp(rms_gain, values_in, gain_row)
    return pull(incoming)


def gelu_pull(values_in, incoming):
    _, pull = jax.vjp(gelu_tanh, values_in)
    return pull(incoming)[0]


def adam_step(weight, first, second, grad, factor, rate, decay):
    grad = grad * factor
    first = beta_one * first + (1.0 - beta_one) * grad
    second = beta_two * second + (1.0 - beta_two) * grad * grad
    first_hat = first / (1.0 - beta_one**STEP)
    second_hat = second / (1.0 - beta_two**STEP)
    weight = weight - rate * (first_hat / (jnp.sqrt(second_hat) + adam_eps) + decay * weight)
    return (weight, first, second)


def on_device(
    inputs,
    dec_in,
    cotangent,
    lengths,
    bucket_table,
    square,
    square_m,
    square_v,
    ffn_in,
    ffn_in_m,
    ffn_in_v,
    ffn_out,
    ffn_out_m,
    ffn_out_v,
    gains,
    gains_m,
    gains_v,
    rel_bias,
    rel_bias_m,
    rel_bias_v,
):
    square_b, ffn_in_b, ffn_out_b, gain_b = (
        lax.all_gather(square.astype(jnp.bfloat16), ("dp", "seq", "head"), axis=1, tiled=True),
        lax.all_gather(ffn_in.astype(jnp.bfloat16), ("dp", "seq", "head"), axis=1, tiled=True),
        lax.all_gather(ffn_out.astype(jnp.bfloat16), ("dp", "seq", "head"), axis=1, tiled=True),
        lax.all_gather(gains.astype(jnp.bfloat16), ("dp", "seq", "head"), axis=1, tiled=True),
    )
    gain_f = gain_b.astype(jnp.float32)
    seq_count = lax.axis_size("seq")
    seq_pos = lax.axis_index("seq")
    row_count, local_len, hidden_width = inputs.shape
    full_span = local_len * seq_count
    heads_here = H // seq_count
    head_cols = hidden_width // seq_count
    bucket_count = rel_bias.shape[0]
    score_scale = 1.0 / math.sqrt(HD)
    first_pos = seq_pos * local_len
    enc_f = inputs.astype(jnp.float32)
    key_valid = jnp.arange(full_span)[None, :] < lengths[:, None]
    offsets = (
        jnp.arange(full_span)[None, :]
        - (first_pos + jnp.arange(local_len))[:, None]
        + full_span
        - 1
    )
    buckets = bucket_table[offsets]
    one_hot_rows = (buckets[None, :, :] == jnp.arange(bucket_count)[:, None, None]).astype(
        jnp.float32
    )

    def bias_lookup(lookup_table_rows):
        return jnp.einsum(
            "top,tr->rop", one_hot_rows, lookup_table_rows, precision=highest_precision
        )

    def encoder_forward():
        normed = rms_gain(enc_f, gain_f[0]).astype(jnp.bfloat16)
        queries = matmul(normed, square_b[0]).astype(jnp.bfloat16)
        keys_here = matmul(normed, square_b[1]).astype(jnp.bfloat16)
        values_here = matmul(normed, square_b[2]).astype(jnp.bfloat16)
        keys_all, values_all = (
            lax.all_gather(keys_here, "seq", axis=1, tiled=True),
            lax.all_gather(values_here, "seq", axis=1, tiled=True),
        )
        query_heads = queries.reshape(row_count, local_len, H, HD)
        key_heads = keys_all.reshape(row_count, full_span, H, HD)
        value_heads = values_all.reshape(row_count, full_span, H, HD)
        raw_scores = jnp.einsum(
            "rqhd,rkhd->rhqk", query_heads, key_heads, preferred_element_type=jnp.float32
        )
        scores = jnp.where(
            key_valid[:, None, None, :],
            raw_scores * score_scale + bias_lookup(rel_bias)[None],
            neg_fill,
        )
        attn_probs = jax.nn.softmax(scores, axis=-1)
        probs_b = attn_probs.astype(jnp.bfloat16)
        attended = (
            jnp.einsum("rhqk,rkhd->rqhd", probs_b, value_heads, preferred_element_type=jnp.float32)
            .reshape(row_count, local_len, hidden_width)
            .astype(jnp.bfloat16)
        )
        hidden = enc_f + matmul(attended, square_b[3])
        normed_two = rms_gain(hidden, gain_f[1]).astype(jnp.bfloat16)
        pre_act = matmul(normed_two, ffn_in_b[0])
        inner_act = gelu_tanh(pre_act).astype(jnp.bfloat16)
        hidden_two = hidden + matmul(inner_act, ffn_out_b[0])
        encoded = rms_gain(hidden_two, gain_f[2]).astype(jnp.bfloat16)
        return (
            normed,
            query_heads,
            key_heads,
            value_heads,
            attn_probs,
            probs_b,
            attended,
            hidden,
            normed_two,
            pre_act,
            inner_act,
            hidden_two,
            encoded,
        )

    first_state = encoder_forward()
    encoded = first_state[12]
    cross_local = jnp.stack(
        (
            matmul(encoded, square_b[7]).astype(jnp.bfloat16),
            matmul(encoded, square_b[8]).astype(jnp.bfloat16),
        ),
        axis=2,
    )
    cross_heads = lax.all_to_all(cross_local, "seq", split_axis=3, concat_axis=1, tiled=True)
    cross_keys = cross_heads[:, :, 0].reshape(row_count, full_span, heads_here, HD)
    cross_values = cross_heads[:, :, 1].reshape(row_count, full_span, heads_here, HD)
    dec_rows = dec_in.reshape(-1, hidden_width).astype(jnp.float32)
    self_norm = rms_gain(dec_rows, gain_f[3]).astype(jnp.bfloat16)
    self_values = matmul(self_norm, square_b[4]).astype(jnp.bfloat16)
    dec_one = dec_rows + matmul(self_values, square_b[5])
    cross_norm = rms_gain(dec_one, gain_f[4]).astype(jnp.bfloat16)
    norms_all = lax.all_gather(cross_norm, "seq", axis=0, tiled=True)
    query_cols = lax.dynamic_slice_in_dim(square_b[6], seq_pos * head_cols, head_cols, 1)
    output_rows = lax.dynamic_slice_in_dim(square_b[9], seq_pos * head_cols, head_cols, 0)
    cross_query = (
        matmul(norms_all, query_cols).astype(jnp.bfloat16).reshape(row_count, heads_here, HD)
    )
    cross_raw = jnp.einsum(
        "rhd,rkhd->rhk", cross_query, cross_keys, preferred_element_type=jnp.float32
    )
    cross_scores = jnp.where(key_valid[:, None, :], cross_raw * score_scale, neg_fill)
    cross_probs = jax.nn.softmax(cross_scores, axis=-1)
    cross_probs_b = cross_probs.astype(jnp.bfloat16)
    cross_att = (
        jnp.einsum("rhk,rkhd->rhd", cross_probs_b, cross_values, preferred_element_type=jnp.float32)
        .reshape(row_count, head_cols)
        .astype(jnp.bfloat16)
    )
    cross_sum = lax.psum_scatter(
        matmul(cross_att, output_rows), "seq", scatter_dimension=0, tiled=True
    )
    dec_two = dec_one + cross_sum
    ffn_norm = rms_gain(dec_two, gain_f[5]).astype(jnp.bfloat16)
    pre_dec = matmul(ffn_norm, ffn_in_b[1])
    inner_dec = gelu_tanh(pre_dec).astype(jnp.bfloat16)
    dec_out = dec_two + matmul(inner_dec, ffn_out_b[1])
    grad_top = cotangent.reshape(-1, hidden_width).astype(jnp.float32)
    grad_top_b = grad_top.astype(jnp.bfloat16)
    grad_inner_dec = matmul(grad_top_b, ffn_out_b[1].T)
    grad_pre_dec = gelu_pull(pre_dec, grad_inner_dec).astype(jnp.bfloat16)
    grad_ffn_norm = matmul(grad_pre_dec, ffn_in_b[1].T)
    grad_two_norm, grad_gain_five = rms_pull(dec_two, gain_f[5], grad_ffn_norm)
    grad_two = grad_top + grad_two_norm
    grad_two_b = grad_two.astype(jnp.bfloat16)
    grad_cross_all = lax.all_gather(grad_two_b, "seq", axis=0, tiled=True)
    grad_att = (
        matmul(grad_cross_all, output_rows.T)
        .astype(jnp.bfloat16)
        .reshape(row_count, heads_here, HD)
    )
    grad_cross_probs = jnp.einsum(
        "rhd,rkhd->rhk", grad_att, cross_values, preferred_element_type=jnp.float32
    )
    grad_cross_values = jnp.einsum(
        "rhk,rhd->rkhd", cross_probs_b, grad_att, preferred_element_type=jnp.float32
    )
    grad_cross_scores = cross_probs * (
        grad_cross_probs - jnp.sum(grad_cross_probs * cross_probs, axis=-1, keepdims=True)
    )
    grad_cross_scores_b = grad_cross_scores.astype(jnp.bfloat16)
    grad_cross_query = (
        (
            jnp.einsum(
                "rhk,rkhd->rhd", grad_cross_scores_b, cross_keys, preferred_element_type=jnp.float32
            )
            * score_scale
        )
        .astype(jnp.bfloat16)
        .reshape(row_count, head_cols)
    )
    grad_cross_keys = (
        jnp.einsum(
            "rhk,rhd->rkhd", grad_cross_scores_b, cross_query, preferred_element_type=jnp.float32
        )
        * score_scale
    )
    gradient_per_head = jnp.stack(
        (
            grad_cross_keys.reshape(row_count, full_span, head_cols),
            grad_cross_values.reshape(row_count, full_span, head_cols),
        ),
        axis=2,
    ).astype(jnp.bfloat16)
    grad_local = lax.all_to_all(gradient_per_head, "seq", split_axis=1, concat_axis=3, tiled=True)
    grad_key_weight = token_outer(encoded, grad_local[:, :, 0])
    grad_value_weight = token_outer(encoded, grad_local[:, :, 1])
    grad_encoded = matmul(grad_local[:, :, 0], square_b[7].T) + matmul(
        grad_local[:, :, 1], square_b[8].T
    )
    grad_norm_part = matmul(grad_cross_query, query_cols.T)
    grad_cross_norm = lax.psum_scatter(grad_norm_part, "seq", scatter_dimension=0, tiled=True)
    grad_one_norm, grad_gain_four = rms_pull(dec_one, gain_f[4], grad_cross_norm)
    grad_one_b = (grad_two + grad_one_norm).astype(jnp.bfloat16)
    grad_self_values = matmul(grad_one_b, square_b[5].T).astype(jnp.bfloat16)
    grad_self_norm = matmul(grad_self_values, square_b[4].T)
    grad_gain_three = rms_pull(dec_rows, gain_f[3], grad_self_norm)[1]
    replay = encoder_forward()
    (
        normed,
        query_heads,
        key_heads,
        value_heads,
        attn_probs,
        probs_b,
        attended,
        hidden,
        normed_two,
        pre_act,
        inner_act,
        hidden_two,
        encoded_again,
    ) = replay
    grad_hidden_two, grad_gain_two = rms_pull(hidden_two, gain_f[2], grad_encoded)
    grad_hidden_two_b = grad_hidden_two.astype(jnp.bfloat16)
    grad_out_enc = token_outer(inner_act, grad_hidden_two_b)
    grad_inner_enc = matmul(grad_hidden_two_b, ffn_out_b[0].T)
    grad_pre_enc = gelu_pull(pre_act, grad_inner_enc).astype(jnp.bfloat16)
    grad_in_enc = token_outer(normed_two, grad_pre_enc)
    grad_normed_two = matmul(grad_pre_enc, ffn_in_b[0].T)
    grad_hidden_norm, grad_gain_one = rms_pull(hidden, gain_f[1], grad_normed_two)
    grad_hidden = grad_hidden_two + grad_hidden_norm
    grad_hidden_b = grad_hidden.astype(jnp.bfloat16)
    grad_enc_out = token_outer(attended, grad_hidden_b)
    grad_attended = (
        matmul(grad_hidden_b, square_b[3].T)
        .astype(jnp.bfloat16)
        .reshape(row_count, local_len, H, HD)
    )
    grad_probs = jnp.einsum(
        "rqhd,rkhd->rhqk", grad_attended, value_heads, preferred_element_type=jnp.float32
    )
    grad_values_all = jnp.einsum(
        "rhqk,rqhd->rkhd", probs_b, grad_attended, preferred_element_type=jnp.float32
    )
    gradient_score_matrix = attn_probs * (
        grad_probs - jnp.sum(grad_probs * attn_probs, axis=-1, keepdims=True)
    )
    grad_bias_here = jnp.einsum(
        "czi,tzi->tc",
        jnp.sum(gradient_score_matrix, axis=0),
        one_hot_rows,
        precision=highest_precision,
    )
    grad_scores_b = gradient_score_matrix.astype(jnp.bfloat16)
    grad_queries = (
        (
            jnp.einsum(
                "rhqk,rkhd->rqhd", grad_scores_b, key_heads, preferred_element_type=jnp.float32
            )
            * score_scale
        )
        .astype(jnp.bfloat16)
        .reshape(row_count, local_len, hidden_width)
    )
    grad_keys_all = (
        jnp.einsum(
            "rhqk,rqhd->rkhd", grad_scores_b, query_heads, preferred_element_type=jnp.float32
        )
        * score_scale
    )
    grad_keys, grad_values = (
        lax.psum_scatter(
            grad_keys_all.reshape(row_count, full_span, hidden_width).astype(jnp.bfloat16),
            "seq",
            scatter_dimension=1,
            tiled=True,
        ).astype(jnp.float32),
        lax.psum_scatter(
            grad_values_all.reshape(row_count, full_span, hidden_width).astype(jnp.bfloat16),
            "seq",
            scatter_dimension=1,
            tiled=True,
        ).astype(jnp.float32),
    )
    grad_keys_b = grad_keys.astype(jnp.bfloat16)
    grad_values_b = grad_values.astype(jnp.bfloat16)
    grad_enc_query = token_outer(normed, grad_queries)
    grad_enc_key = token_outer(normed, grad_keys_b)
    grad_enc_value = token_outer(normed, grad_values_b)
    grad_normed = (
        matmul(grad_queries, square_b[0].T)
        + matmul(grad_keys_b, square_b[1].T)
        + matmul(grad_values_b, square_b[2].T)
    )
    grad_input_norm, grad_gain_zero = rms_pull(enc_f, gain_f[0], grad_normed)
    input_grad = grad_hidden + grad_input_norm
    grad_gains = jnp.stack(
        (
            grad_gain_zero,
            grad_gain_one,
            grad_gain_two,
            grad_gain_three,
            grad_gain_four,
            grad_gain_five,
        )
    )
    grad_out_dec = matmul(inner_dec.T, grad_top_b)
    grad_in_dec = matmul(ffn_norm.T, grad_pre_dec)
    grad_out_rows = matmul(cross_att.T, grad_cross_all)
    grad_query_cols = matmul(norms_all.T, grad_cross_query)
    grad_self_out = matmul(self_values.T, grad_one_b)
    grad_self_in = matmul(self_norm.T, grad_self_values)
    zero_square = jnp.zeros((hidden_width, hidden_width), jnp.float32)
    grad_query_full = lax.dynamic_update_slice_in_dim(
        zero_square, grad_query_cols, seq_pos * head_cols, 1
    )
    grad_rows_full = lax.dynamic_update_slice_in_dim(
        zero_square, grad_out_rows, seq_pos * head_cols, 0
    )
    part_square = jnp.stack(
        (
            grad_enc_query,
            grad_enc_key,
            grad_enc_value,
            grad_enc_out,
            grad_self_in,
            grad_self_out,
            grad_query_full,
            grad_key_weight,
            grad_value_weight,
            grad_rows_full,
        )
    )
    part_in = jnp.stack((grad_in_enc, grad_in_dec))
    part_out = jnp.stack((grad_out_enc, grad_out_dec))
    summed_part, summed_part_in, summed_part_out, summed_gain = (
        lax.psum_scatter(part_square, ("dp", "seq", "head"), scatter_dimension=1, tiled=True),
        lax.psum_scatter(part_in, ("dp", "seq", "head"), scatter_dimension=1, tiled=True),
        lax.psum_scatter(part_out, ("dp", "seq", "head"), scatter_dimension=1, tiled=True),
        lax.psum_scatter(grad_gains, ("dp", "seq", "head"), scatter_dimension=1, tiled=True),
    )
    local_squares = (
        jnp.sum(summed_part * summed_part)
        + jnp.sum(summed_part_in * summed_part_in)
        + jnp.sum(summed_part_out * summed_part_out)
        + jnp.sum(summed_gain * summed_gain)
    )
    grad_bias, shard_squares = lax.psum((grad_bias_here, local_squares), ("dp", "seq", "head"))
    grad_norm = jnp.sqrt(shard_squares + jnp.sum(grad_bias * grad_bias))
    factor = clip_bound / jnp.maximum(grad_norm, clip_bound)
    square_new, square_m_new, square_v_new = adam_step(
        square, square_m, square_v, summed_part, factor, rate_matrix, decay_rate
    )
    ffn_in_new, ffn_in_m_new, ffn_in_v_new = adam_step(
        ffn_in, ffn_in_m, ffn_in_v, summed_part_in, factor, rate_matrix, decay_rate
    )
    ffn_out_new, ffn_out_m_new, ffn_out_v_new = adam_step(
        ffn_out, ffn_out_m, ffn_out_v, summed_part_out, factor, rate_matrix, decay_rate
    )
    gains_new, gains_m_new, gains_v_new = adam_step(
        gains, gains_m, gains_v, summed_gain, factor, rate_small, 0.0
    )
    rel_bias_new, rel_bias_m_new, rel_bias_v_new = adam_step(
        rel_bias, rel_bias_m, rel_bias_v, grad_bias, factor, rate_small, 0.0
    )
    return (
        dec_out.astype(jnp.bfloat16).reshape(dec_in.shape),
        input_grad,
        grad_norm,
        square_new,
        square_m_new,
        square_v_new,
        ffn_in_new,
        ffn_in_m_new,
        ffn_in_v_new,
        ffn_out_new,
        ffn_out_m_new,
        ffn_out_v_new,
        gains_new,
        gains_m_new,
        gains_v_new,
        rel_bias_new,
        rel_bias_m_new,
        rel_bias_v_new,
    )


def solution(mesh):
    placed = (
        P(("dp", "head"), "seq", None),
        P(("dp", "head"), "seq", None),
        P(("dp", "head"), "seq", None),
        P(("dp", "head")),
        P(),
        P(None, ("dp", "seq", "head"), None),
        P(None, ("dp", "seq", "head"), None),
        P(None, ("dp", "seq", "head"), None),
        P(None, ("dp", "seq", "head"), None),
        P(None, ("dp", "seq", "head"), None),
        P(None, ("dp", "seq", "head"), None),
        P(None, ("dp", "seq", "head"), None),
        P(None, ("dp", "seq", "head"), None),
        P(None, ("dp", "seq", "head"), None),
        P(None, ("dp", "seq", "head")),
        P(None, ("dp", "seq", "head")),
        P(None, ("dp", "seq", "head")),
        P(),
        P(),
        P(),
    )
    return jax.shard_map(
        on_device,
        mesh=mesh,
        in_specs=placed,
        out_specs=(
            P(("dp", "head"), "seq", None),
            P(("dp", "head"), "seq", None),
            P(),
            P(None, ("dp", "seq", "head"), None),
            P(None, ("dp", "seq", "head"), None),
            P(None, ("dp", "seq", "head"), None),
            P(None, ("dp", "seq", "head"), None),
            P(None, ("dp", "seq", "head"), None),
            P(None, ("dp", "seq", "head"), None),
            P(None, ("dp", "seq", "head"), None),
            P(None, ("dp", "seq", "head"), None),
            P(None, ("dp", "seq", "head"), None),
            P(None, ("dp", "seq", "head")),
            P(None, ("dp", "seq", "head")),
            P(None, ("dp", "seq", "head")),
            P(),
            P(),
            P(),
        ),
        check_vma=False,
    )
```

profile of v0, /device:TPU:0, one launch (start us, length us, event | category | flops | bytes accessed | tf_op | source)
XLA Modules:
  0.0 1466.3 jit_solution(9738038624949049584)
XLA Ops:
  12.0 43.9 %all-gather = bf16[32,24,6]{1,2,0:T(8,128)(2,1)S(1)} all-gather(bf16[1,24,6]{1,2,0:T(8,128)(2,1)S(1)} %convert_bitcast_fusion.3), channel_id=1, replica_groups=mesh['dp'=4,'seq'=4,'head'=2] {'dp','seq','head'}, dimensions={0}, use_global_device_ids=true | all-gather | bytes 9504 | tf_op jit(solution)/shard_map/all_gather | solution.py:91
  58.9 47.9 %all-gather.9.cloned.1.call-done = bf16[10,768,768]{2,1,0:T(8,128)(2,1)} async-done(((bf16[10,24,768]{2,1,0:T(8,128)(2,1)}), bf16[10,768,768]{2,1,0:T(8,128)(2,1)}) %all-gather.9.cloned.1.call-update) | async-done | bytes 11796496 | tf_op jit(solution)/shard_map/all_gather | solution.py:88
  111.4 3.0 convolution_convert_fusion.3
  114.5 3.1 convolution_convert_fusion.5
  120.0 260.7 %gather_fusion = s32[65536]{0:T(1024)S(1)} fusion(s32[1023]{0:T(1024)S(1)} %copy-done, s32[65536]{0:T(1024)S(1)} %broadcast_clamp_fusion), kind=kCustom, calls=%fused_computation | custom fusion | bytes 786432 | tf_op jit(solution)/shard_map/gather | solution.py:111
  382.1 37.3 %copy.154 = pred[32,128,512]{2,0,1:T(32,128)(4,1)S(1)} copy(pred[32,128,512]{1,0,2:T(32,128)(4,1)S(1)} %iota_compare_fusion) | data formatting | bytes 4194304 | tf_op jit(solution)/shard_map/eq | solution.py:112
  419.4 2.5 convolution_bitcast_fusion.2
  421.9 3.5 copy.155
  428.7 3.2 copy.152
  431.9 5.6 copy.150
  437.6 11.6 fusion.152
  449.1 8.0 fusion.42
  457.1 2.5 multiply_reduce_fusion.6
  459.7 7.1 fusion.19
  466.8 8.0 multiply_reduce_fusion.5
  475.1 2.3 fusion.46
  480.7 3.8 copy.157
  484.5 4.3 all-to-all-start
  489.5 3.7 fusion.24
  493.2 17.3 %all-gather.1 = bf16[4,1,768]{2,1,0:T(2,128)(2,1)S(1)} all-gather(bf16[1,1,768]{2,1,0:T(2,128)(2,1)S(1)} %get-tuple-element.70), channel_id=1, replica_groups=mesh['dp'=4,'seq'=4,'head'=2] {'seq'}, dimensions={0}, use_global_device_ids=true | all-gather | bytes 7680 | tf_op jit(solution)/shard_map/all_gather | solution.py:187
  510.5 2.8 fusion.150
  521.7 16.6 %all-reduce = f32[4,768]{1,0:T(4,128)S(1)} all-reduce(f32[4,768]{1,0:T(4,128)S(1)} %fusion.75), channel_id=2, replica_groups=mesh['dp'=4,'seq'=4,'head'=2] {'seq'}, use_global_device_ids=true, to_apply=%region_9.10.clone | all-reduce | flops 3072 | bytes 24576
  540.3 3.1 fusion.23
  543.4 4.8 multiply_multiply_fusion.13
  548.9 7.2 all-gather.2
  560.6 6.2 copy.160
  566.8 23.5 %all_to_all.36 = bf16[4,512,2,192]{3,2,0,1:T(2,128)(2,1)} all-to-all(bf16[4,512,2,192]{3,2,0,1:T(2,128)(2,1)} %copy.160), channel_id=1, replica_groups=mesh['dp'=4,'seq'=4,'head'=2] {'seq'}, dimensions={1} | all-to-all | bytes 3145728 | tf_op jit(solution)/shard_map/all_to_all | solution.py:259
  590.3 6.4 copy.198
  598.7 2.7 fusion.61
  601.4 2.6 multiply_reduce_fusion.1
  604.5 8.4 fusion.11
  613.0 2.8 multiply_reduce_fusion.2
  619.9 12.4 multiply_reduce_fusion
  632.8 8.4 fusion.16
  641.1 3.2 multiply_convert_fusion
  644.7 4.6 copy.167
  649.4 7.4 fusion.30
  656.8 4.8 copy.168
  663.6 2.8 convolution_bitcast_fusion.1
  666.3 6.8 pad_maximum_fusion
  674.7 5.4 convolution_bitcast_fusion
  680.1 6.7 pad_maximum_fusion.1
  689.8 14.5 all-reduce.1
  711.6 5.1 dynamic_update_slice.8
  719.3 5.2 multiply_convert_fusion.2
  725.4 2.4 bitcast_dynamic-update-slice_fusion.7
  727.8 3.4 bitcast_dynamic-update-slice_fusion.6
  731.3 7.1 reduce-scatter.9.cloned.1.call-done
  738.4 3.5 bitcast_dynamic-update-slice_fusion.5
  749.0 2.2 bitcast_dynamic-update-slice_fusion.1
  753.5 3.5 constant_dynamic-update-slice_fusion
  758.9 4.0 fusion.56
  762.9 5.3 copy.178
  768.3 7.2 convolution_bitcast_fusion.5
  775.5 2.3 fusion.59
  780.1 3.7 fusion.36
  783.8 41.5 %all-reduce.2 = f32[6,768]{1,0:T(8,128)S(1)} all-reduce(f32[6,768]{1,0:T(8,128)S(1)} %stack.103), channel_id=9, replica_groups=mesh['dp'=4,'seq'=4,'head'=2] {'dp','seq','head'}, use_global_device_ids=true, to_apply=%region_30.31.clone | all-reduce | flops 4608 | bytes 36864
  826.6 123.8 %reduce-scatter.13.cloned.1.call-done = f32[2,24,3072]{2,1,0:T(8,128)} async-done(((f32[2,768,3072]{2,1,0:T(8,128)}), f32[2,24,3072]{2,1,0:T(8,128)}) %reduce-scatter.13.cloned.1.call-update) | async-done | bytes 589840 | tf_op jit(solution)/shard_map/reduce_scatter | solution.py:403
  952.2 208.6 %reduce-scatter.15.cloned.1.call-done = f32[2,96,768]{2,1,0:T(8,128)} async-done(((f32[2,3072,768]{2,1,0:T(8,128)}), f32[2,96,768]{2,1,0:T(8,128)}) %reduce-scatter.15.cloned.1.call-update) | async-done | bytes 589840 | tf_op jit(solution)/shard_map/reduce_scatter | solution.py:404
  1162.7 235.2 %reduce-scatter.11.cloned.1.call-done = f32[10,24,768]{2,1,0:T(8,128)} async-done(((f32[10,768,768]{2,1,0:T(8,128)}), f32[10,24,768]{2,1,0:T(8,128)}) %reduce-scatter.11.cloned.1.call-update) | async-done | bytes 737296 | tf_op jit(solution)/shard_map/reduce_scatter | solution.py:402
  1402.4 3.0 fusion.38
  1405.4 40.3 %all-reduce.3 = (f32[]{:T(128)}, f32[32,12]{0,1:T(8,128)S(1)}) all-reduce(f32[]{:T(128)S(6)} %add.314, f32[32,12]{0,1:T(8,128)} %convolution_bitcast_fusion.5), channel_id=1, replica_groups=mesh['dp'=4,'seq'=4,'head'=2] {'dp','seq','head'}, use_global_device_ids=true, to_apply=%region_32.33 | all-reduce | flops 385 | bytes 3080 | tf_op jit(solution)/shard_map/psum | solution.py:413
  1450.5 2.9 multiply_subtract_fusion.1
  1453.4 2.8 multiply_subtract_fusion.2
  (286 shorter events, 85.6 us)
Async XLA Ops:
  7.2 112.8 %copy-start = (s32[1023]{0:T(1024)S(1)}, s32[1023]{0:T(1024)}, u32[]{:S(2)}) copy-start(s32[1023]{0:T(1024)} %param.24) | copy-start | bytes 12280
  7.2 104.2 %copy-start.7 = (bf16[4,128,768]{2,1,0:T(8,128)(2,1)S(1)}, bf16[4,128,768]{2,1,0:T(8,128)(2,1)}, u32[]{:S(2)}) copy-start(bf16[4,128,768]{2,1,0:T(8,128)(2,1)} %param.20) | copy-start | bytes 2359300
  7.2 99.6 %all-gather.9.cloned.1.call-start = ((), (), s32[]{:S(2)}) async-start(), calls=%async_computation.7 | async-start | bytes 12165120 | tf_op jit(solution)/shard_map/all_gather | solution.py:88
  9.2 419.5 %all-gather.13.cloned.1.call-start = ((), (), s32[]{:S(2)}) async-start(), calls=%async_computation.9 | async-start | bytes 3932160 | tf_op jit(solution)/shard_map/all_gather | solution.py:127
  10.6 103.8 %copy-start.42 = (f32[768]{0:T(1024)}, f32[768]{0:T(1024)S(1)}, u32[]{:S(2)}) copy-start(f32[768]{0:T(1024)S(1)} %get-tuple-element.28) | copy-start | bytes 9220
  57.6 56.8 %copy-start.51 = (f32[4,128]{1,0:T(4,128)}, f32[4,128]{1,0:T(4,128)S(1)}, u32[]{:S(2)}) copy-start(f32[4,128]{1,0:T(4,128)S(1)} %fusion.39) | copy-start | bytes 6148
  57.6 367.9 %copy-start.55 = (f32[4,128]{1,0:T(4,128)}, f32[4,128]{1,0:T(4,128)S(1)}, u32[]{:S(2)}) copy-start(f32[4,128]{1,0:T(4,128)S(1)} %fusion.121) | copy-start | bytes 6148
  108.4 6.0 copy-start.53
  111.3 6.2 copy-start.44
  111.4 314.1 %copy-start.46 = (f32[768]{0:T(1024)}, f32[768]{0:T(1024)S(1)}, u32[]{:S(2)}) copy-start(f32[768]{0:T(1024)S(1)} %get-tuple-element.26) | copy-start | bytes 9220
  114.4 4.6 copy-start.28
  114.4 317.5 %all-gather.11.cloned.1.call-start = ((), (), s32[]{:S(2)}) async-start(), calls=%async_computation.8 | async-start | bytes 3932160 | tf_op jit(solution)/shard_map/all_gather | solution.py:128
  117.6 342.1 %all-gather.15.cloned.1.call-start = ((), (), s32[]{:S(2)}) async-start(), calls=%async_computation.10 | async-start | bytes 9732096 | tf_op jit(solution)/shard_map/all_gather | solution.py:89
  118.4 348.4 %all-gather.17.cloned.1.call-start = ((), (), s32[]{:S(2)}) async-start(), calls=%async_computation.11 | async-start | bytes 9732096 | tf_op jit(solution)/shard_map/all_gather | solution.py:90
  380.9 38.5 %copy-start.34 = (s32[128,512]{0,1:T(8,128)}, s32[128,512]{0,1:T(8,128)S(1)}, u32[]{:S(2)}) copy-start(s32[128,512]{0,1:T(8,128)S(1)} %copy.153) | copy-start | bytes 786436
  380.9 38.5 %copy-start.48 = (f32[32,12]{0,1:T(8,128)S(1)}, f32[32,12]{0,1:T(8,128)}, u32[]{:S(2)}) copy-start(f32[32,12]{0,1:T(8,128)} %param.37) | copy-start | bytes 4612
  421.9 3.5 copy-start.60
  431.9 5.6 copy-start.3
  449.1 8.0 copy-start.8
  480.7 8.2 copy-start.62
  480.7 8.8 copy-start.50
  484.5 30.4 %all-to-all-start = ((bf16[4,128,2,768]{1,0,2,3:T(4,128)(2,1)}), bf16[4,128,2,768]{1,0,2,3:T(4,128)(2,1)}, u32[]{:S(2)}, u32[]{:S(2)}) async-start(bf16[4,128,2,768]{1,0,2,3:T(4,128)(2,1)} %copy.157), calls=%async_computation | async-start | bytes 3145728 | tf_op jit(solution)/shard_map/all_to_all | solution.py:179
  488.9 238.9 %reduce-scatter.7.cloned.1.call-start = ((), (), s32[]{:S(2)}) async-start(), calls=%async_computation.12 | async-start | bytes 3932160 | tf_op jit(solution)/shard_map/reduce_scatter | solution.py:337
  596.7 7.7 slice-start.3
  598.7 5.4 copy-start.11
  598.7 5.7 slice-start.4
  604.0 8.9 slice-start.6
  604.4 11.4 copy-start.16
  604.5 8.5 slice-start.7
  604.5 8.5 slice-start.8
  619.9 12.5 slice-start
  619.9 12.5 slice-start.1
  619.9 12.8 slice-start.2
  632.8 8.4 copy-start.19
  641.1 3.6 copy-start.2
  649.3 89.0 %reduce-scatter.9.cloned.1.call-start = ((), (), s32[]{:S(2)}) async-start(), calls=%async_computation.13 | async-start | bytes 3932160 | tf_op jit(solution)/shard_map/reduce_scatter | solution.py:343
  661.6 288.8 %reduce-scatter.13.cloned.1.call-start = ((), (), s32[]{:S(2)}) async-start(), calls=%async_computation.15 | async-start | bytes 19464192 | tf_op jit(solution)/shard_map/reduce_scatter | solution.py:403
  673.1 487.7 %reduce-scatter.15.cloned.1.call-start = ((), (), s32[]{:S(2)}) async-start(), calls=%async_computation.16 | async-start | bytes 19464192 | tf_op jit(solution)/shard_map/reduce_scatter | solution.py:404
  686.8 17.5 %copy-start.45 = (f32[768]{0:T(1024)S(1)}, f32[768]{0:T(1024)}, u32[]{:S(2)}) copy-start(f32[768]{0:T(1024)} %copy-done.44) | copy-start | bytes 9220
  686.8 711.1 %reduce-scatter.11.cloned.1.call-start = ((), (), s32[]{:S(2)}) async-start(), calls=%async_computation.14 | async-start | bytes 24330240 | tf_op jit(solution)/shard_map/reduce_scatter | solution.py:402
  709.9 9.4 copy-start.4
  719.3 6.1 copy-start.9
  719.3 6.1 copy-start.47
  719.3 6.1 copy-start.56
  731.3 10.6 copy-start.6
  731.3 10.6 copy-start.25
  762.9 5.4 copy-start.35
  768.3 7.2 copy-start.37
  768.3 9.6 copy-start.61
  775.5 4.6 copy-start.38
  780.1 3.7 copy-start.58
  780.1 45.9 %copy-start.52 = (f32[4,128]{1,0:T(4,128)S(1)}, f32[4,128]{1,0:T(4,128)}, u32[]{:S(2)}) copy-start(f32[4,128]{1,0:T(4,128)} %copy-done.51) | copy-start | bytes 6148
  825.3 335.6 %copy-start.41 = (f32[6,768]{1,0:T(8,128)}, f32[6,768]{1,0:T(8,128)S(1)}, u32[]{:S(2)}) copy-start(f32[6,768]{1,0:T(8,128)S(1)} %all-reduce.2) | copy-start | bytes 55300
  1162.7 285.0 %copy-start.57 = (f32[6,24]{1,0:T(8,128)S(1)}, f32[6,24]{1,0:T(8,128)}, u32[]{:S(2)}) copy-start(f32[6,24]{1,0:T(8,128)} %param.34) | copy-start | bytes 1732
  1162.7 286.4 %copy-start.49 = (f32[32,12]{0,1:T(8,128)S(1)}, f32[32,12]{0,1:T(8,128)}, u32[]{:S(2)}) copy-start(f32[32,12]{0,1:T(8,128)} %param.37) | copy-start | bytes 4612
  1162.7 287.8 %copy-start.29 = (f32[2,96,768]{2,1,0:T(8,128)S(1)}, f32[2,96,768]{2,1,0:T(8,128)}, u32[]{:S(2)}) copy-start(f32[2,96,768]{2,1,0:T(8,128)} %param.31) | copy-start | bytes 1769476
  1162.7 287.8 %copy-start.33 = (f32[2,96,768]{2,1,0:T(8,128)S(1)}, f32[2,96,768]{2,1,0:T(8,128)}, u32[]{:S(2)}) copy-start(f32[2,96,768]{2,1,0:T(8,128)} %reduce-scatter.15.cloned.1.call-done) | copy-start | bytes 1769476
  1405.4 48.0 %copy-start.31 = (f32[2,24,3072]{2,1,0:T(8,128)S(1)}, f32[2,24,3072]{2,1,0:T(8,128)}, u32[]{:S(2)}) copy-start(f32[2,24,3072]{2,1,0:T(8,128)} %param.28) | copy-start | bytes 1769476
  1405.4 48.0 %copy-start.32 = (f32[2,24,3072]{2,1,0:T(8,128)S(1)}, f32[2,24,3072]{2,1,0:T(8,128)}, u32[]{:S(2)}) copy-start(f32[2,24,3072]{2,1,0:T(8,128)} %reduce-scatter.13.cloned.1.call-done) | copy-start | bytes 1769476
  1450.5 5.8 copy-start.26
  1450.5 5.8 copy-start.27
  1450.5 5.8 copy-start.39
  1450.5 5.8 copy-start.40
  1453.4 4.6 copy-start.1
  (19 other events, 39.2 us)
Sparse Core Ops, SparseCore 0:
  11.6 95.2 all-gather.8
  114.5 42.2 all-gather.12
  159.3 43.9 all-gather.10
  206.7 82.0 all-gather.14
  292.1 80.6 all-gather.16
  649.5 41.8 reduce-scatter.6
  694.3 43.9 reduce-scatter.8
  744.8 205.5 reduce-scatter.12
  956.8 204.0 reduce-scatter.14
  1167.1 230.7 reduce-scatter.10
where the time goes:
time: 1470 us
  waiting for transfers between devices  623 us (42%)
  local copies, waits for them, and re-layouts  373 us (25%)
  blocking collectives  205 us (14%)
  matrix products  171 us (12%)
  other arithmetic  65.3 us (4%)
  between operations  24.2 us (2%)
    gather x3, local copies, waits for them, and re-layouts, on_device(): buckets = bucket_table[offsets]  261 us
    reduce_scatter x1, waiting for transfers between devices, on_device(): lax.psum_scatter(part_square, ('dp', 'seq', 'head'), scatter_dimension=1,...  235 us
    reduce_scatter x1, waiting for transfers between devices, on_device(): lax.psum_scatter(part_out, ('dp', 'seq', 'head'), scatter_dimension=1, ti...  209 us
    reduce_scatter x1, waiting for transfers between devices, on_device(): lax.psum_scatter(part_in, ('dp', 'seq', 'head'), scatter_dimension=1, til...  124 us
    dot_general x30, matrix products, matmul(): return jnp.dot(left, right, preferred_element_type=jnp.float32)  85.5 us
    unnamed x3, blocking collectives  72.6 us
    all_gather x1, waiting for transfers between devices, on_device(): lax.all_gather(square.astype(jnp.bfloat16), ('dp', 'seq', 'head'), axis=1...  47.9 us
    all_gather x1, blocking collectives, on_device(): lax.all_gather(gains.astype(jnp.bfloat16), ('dp', 'seq', 'head'), axis=1,...  43.9 us
  transfers between devices with their start and end apart: 11, of which 5 were waited for; matrix products, arithmetic and copies ran while one was open for 33% of the time, Pallas kernels for 0%

commit v1 on v0

v1 whole, which is shorter than its diff:
```python
import functools
import math

import jax
import jax.numpy as jnp
from jax import lax
from jax.experimental import pallas as pl
from jax.experimental.pallas import tpu as pltpu
from jax.sharding import PartitionSpec as P

H = 12
HD = 64
STEP = 5
AXES = ("dp", "seq", "head")

norm_eps = 1e-06
neg_fill = -1e30
beta_one = 0.9
beta_two = 0.999
adam_eps = 1e-08
decay_rate = 0.01
rate_matrix = 0.05
rate_small = 0.5
clip_bound = 1.0
highest_precision = lax.Precision.HIGHEST
bf16 = jnp.bfloat16
f32 = jnp.float32
BAND = 128


def rms_gain(values_in, gain_row):
    return (
        values_in
        * lax.rsqrt(jnp.mean(values_in * values_in, axis=-1, keepdims=True) + norm_eps)
        * gain_row
    )


def gelu_tanh(values_in):
    return jax.nn.gelu(values_in, approximate=True)


def matmul(left, right):
    return jnp.dot(left, right, preferred_element_type=f32)


def mm_t(left, right):
    return lax.dot_general(left, right, (((1,), (1,)), ((), ())), preferred_element_type=f32)


def mm_outer(left, right):
    return lax.dot_general(left, right, (((0,), (0,)), ((), ())), preferred_element_type=f32)


def rms_pull(values_in, gain_row, incoming):
    _, pull = jax.vjp(rms_gain, values_in, gain_row)
    return pull(incoming)


def gelu_pull(values_in, incoming):
    _, pull = jax.vjp(gelu_tanh, values_in)
    return pull(incoming)[0]


def adam_step(weight, first, second, grad, factor, rate, decay):
    grad = grad * factor
    first = beta_one * first + (1.0 - beta_one) * grad
    second = beta_two * second + (1.0 - beta_two) * grad * grad
    first_hat = first / (1.0 - beta_one**STEP)
    second_hat = second / (1.0 - beta_two**STEP)
    weight = weight - rate * (first_hat / (jnp.sqrt(second_hat) + adam_eps) + decay * weight)
    return (weight, first, second)


def bias_band(table_row, span):
    wide = jnp.broadcast_to(table_row, (BAND, 2 * span))
    shift = (2 * span - (BAND - 1)) % (2 * span)
    return pltpu.roll(wide, shift, 1, stride=1, stride_axis=0)


def band_sums(band, span):
    wide = 2 * span
    rows = BAND
    while rows > 8:
        rows //= 2
        band = band[:rows] + pltpu.roll(band[rows:], wide - rows, 1)
    row = lax.broadcasted_iota(jnp.int32, band.shape, 0)
    for step in (4, 2, 1):
        band = jnp.where((row // step) % 2 == 1, pltpu.roll(band, wide - step, 1), band)
    return pltpu.roll(jnp.sum(band, axis=0, keepdims=True), BAND - 1, 1)


def softmax_rows(q_rows, k_all, band, block, span, valid):
    start = span - BAND * (block + 1)
    scores = mm_t(q_rows, k_all) * (1.0 / math.sqrt(HD)) + band[:, start : start + span]
    scores = jnp.where(valid, scores, neg_fill)
    peak = jnp.max(scores, axis=-1, keepdims=True)
    raised = jnp.exp(scores - peak)
    return raised / jnp.sum(raised, axis=-1, keepdims=True)


def attend_fwd_kernel(len_ref, table_ref, q_ref, k_ref, v_ref, o_ref):
    span = k_ref.shape[0]
    valid = lax.broadcasted_iota(jnp.int32, (1, span), 1) < len_ref[0]
    lane = lax.broadcasted_iota(jnp.int32, (1, 2 * HD), 1)
    k_all = k_ref[...]
    v_all = v_ref[...]
    bands = [bias_band(table_ref[t], span) for t in range(2)]
    for block in range(span // BAND):
        rows = slice(block * BAND, (block + 1) * BAND)
        q_rows = q_ref[rows, :]
        parts = []
        for t in range(2):
            own = (lane // HD) == t
            probs = softmax_rows(
                jnp.where(own, q_rows, jnp.zeros_like(q_rows)), k_all, bands[t], block, span, valid
            )
            parts.append(matmul(probs.astype(bf16), v_all))
        o_ref[rows, :] = jnp.where(lane < HD, parts[0], parts[1]).astype(bf16)


def attend_bwd_kernel(
    len_ref, table_ref, q_ref, k_ref, v_ref, do_ref, dq_ref, dk_ref, dv_ref, dt_ref
):
    span = k_ref.shape[0]
    scale = 1.0 / math.sqrt(HD)
    valid = lax.broadcasted_iota(jnp.int32, (1, span), 1) < len_ref[0]
    lane = lax.broadcasted_iota(jnp.int32, (1, 2 * HD), 1)
    k_all = k_ref[...]
    v_all = v_ref[...]
    count = span // BAND
    dks, dvs = [], []
    dqs = [[None, None] for _ in range(count)]
    for t in range(2):
        own = (lane // HD) == t
        band = bias_band(table_ref[t], span)
        dk = jnp.zeros((span, 2 * HD), f32)
        dv = jnp.zeros((span, 2 * HD), f32)
        dband = jnp.zeros((BAND, 2 * span), f32)
        for block in range(count):
            rows = slice(block * BAND, (block + 1) * BAND)
            q_rows = q_ref[rows, :]
            do_rows = do_ref[rows, :]
            zero = jnp.zeros_like(q_rows)
            probs = softmax_rows(
                jnp.where(own, q_rows, zero), k_all, band, block, span, valid
            )
            dprobs = mm_t(jnp.where(own, do_rows, zero), v_all)
            dscore = probs * (dprobs - jnp.sum(dprobs * probs, axis=-1, keepdims=True))
            start = span - BAND * (block + 1)
            pieces = []
            if start:
                pieces.append(jnp.zeros((BAND, start), f32))
            pieces.append(dscore)
            if span - start:
                pieces.append(jnp.zeros((BAND, span - start), f32))
            dband = dband + jnp.concatenate(pieces, axis=1)
            dscore_b = dscore.astype(bf16)
            dv = dv + mm_outer(probs.astype(bf16), do_rows)
            dk = dk + mm_outer(dscore_b, q_rows)
            dqs[block][t] = matmul(dscore_b, k_all)
        dks.append(dk)
        dvs.append(dv)
        dt_ref[t] = band_sums(dband, span)
    dk_ref[...] = (jnp.where(lane < HD, dks[0], dks[1]) * scale).astype(bf16)
    dv_ref[...] = jnp.where(lane < HD, dvs[0], dvs[1]).astype(bf16)
    for block in range(count):
        rows = slice(block * BAND, (block + 1) * BAND)
        dq_ref[rows, :] = (jnp.where(lane < HD, dqs[block][0], dqs[block][1]) * scale).astype(bf16)


def head_specs(span, width, n):
    return [pl.BlockSpec((span, 2 * HD), lambda i: (0, i)) for _ in range(n)]


def attend_fwd(length, table, q, k, v):
    span, width = q.shape
    return pl.pallas_call(
        attend_fwd_kernel,
        grid=(width // (2 * HD),),
        out_shape=jax.ShapeDtypeStruct((span, width), bf16),
        in_specs=[
            pl.BlockSpec(memory_space=pltpu.SMEM),
            pl.BlockSpec((2, 1, 2 * span), lambda i: (i, 0, 0)),
            *head_specs(span, width, 3),
        ],
        out_specs=head_specs(span, width, 1)[0],
        compiler_params=pltpu.CompilerParams(vmem_limit_bytes=48 * 1024 * 1024),
        name="attend_fwd",
    )(length, table, q, k, v)


def attend_bwd(length, table, q, k, v, do):
    span, width = q.shape
    like = jax.ShapeDtypeStruct((span, width), bf16)
    return pl.pallas_call(
        attend_bwd_kernel,
        grid=(width // (2 * HD),),
        out_shape=(like, like, like, jax.ShapeDtypeStruct(table.shape, f32)),
        in_specs=[
            pl.BlockSpec(memory_space=pltpu.SMEM),
            pl.BlockSpec((2, 1, 2 * span), lambda i: (i, 0, 0)),
            *head_specs(span, width, 4),
        ],
        out_specs=(
            *head_specs(span, width, 3),
            pl.BlockSpec((2, 1, 2 * span), lambda i: (i, 0, 0)),
        ),
        compiler_params=pltpu.CompilerParams(vmem_limit_bytes=48 * 1024 * 1024),
        name="attend_bwd",
    )(length, table, q, k, v, do)


def on_device(
    inputs,
    dec_in,
    cotangent,
    lengths,
    bucket_table,
    square,
    square_m,
    square_v,
    ffn_in,
    ffn_in_m,
    ffn_in_v,
    ffn_out,
    ffn_out_m,
    ffn_out_v,
    gains,
    gains_m,
    gains_v,
    rel_bias,
    rel_bias_m,
    rel_bias_v,
):
    def gather_rows(x):
        return lax.all_gather(x.astype(bf16), AXES, axis=x.ndim - 2, tiled=True)

    sq_a = gather_rows(square[:4])
    w_in_e = gather_rows(ffn_in[0])
    w_out_e = gather_rows(ffn_out[0])
    sq_b = gather_rows(jnp.stack([square[i] for i in (7, 8, 4, 5, 6, 9)]))
    w_in_d = gather_rows(ffn_in[1])
    w_out_d = gather_rows(ffn_out[1])
    gain_f = lax.all_gather(gains.astype(bf16), AXES, axis=1, tiled=True).astype(f32)
    w = {0: sq_a[0], 1: sq_a[1], 2: sq_a[2], 3: sq_a[3]}
    for n, i in enumerate((7, 8, 4, 5, 6, 9)):
        w[i] = sq_b[n]

    seq_pos = lax.axis_index("seq")
    local_len, width = inputs.shape[1:]
    span = local_len * lax.axis_size("seq")
    bucket_count = rel_bias.shape[0]
    scale = 1.0 / math.sqrt(HD)
    x_b = lax.all_to_all(inputs, "seq", split_axis=0, concat_axis=1, tiled=True)[0]
    x_f = x_b.astype(f32)
    length = lax.dynamic_slice_in_dim(lengths, seq_pos, 1, 0)
    key_valid = jnp.arange(span)[None, :] < length[:, None]
    one_hot = (
        jnp.pad(bucket_table, (0, 1), constant_values=-1)[:, None]
        == jnp.arange(bucket_count)[None, :]
    ).astype(f32)
    table = jnp.einsum("ob,bh->ho", one_hot, rel_bias, precision=highest_precision)[:, None, :]

    normed = rms_gain(x_f, gain_f[0]).astype(bf16)
    q = matmul(normed, w[0]).astype(bf16)
    k = matmul(normed, w[1]).astype(bf16)
    v = matmul(normed, w[2]).astype(bf16)
    attended = attend_fwd(length, table, q, k, v)
    hidden = x_f + matmul(attended, w[3])
    normed_two = rms_gain(hidden, gain_f[1]).astype(bf16)
    pre_act = matmul(normed_two, w_in_e)
    inner_act = gelu_tanh(pre_act).astype(bf16)
    hidden_two = hidden + matmul(inner_act, w_out_e)
    encoded = rms_gain(hidden_two, gain_f[2]).astype(bf16)
    cross_k = matmul(encoded, w[7]).astype(bf16)
    cross_v = matmul(encoded, w[8]).astype(bf16)

    dec_row = dec_in.reshape(1, width).astype(f32)
    self_norm = rms_gain(dec_row, gain_f[3]).astype(bf16)
    self_values = matmul(self_norm, w[4]).astype(bf16)
    dec_one = dec_row + matmul(self_values, w[5])
    cross_norm = rms_gain(dec_one, gain_f[4]).astype(bf16)
    cross_q = matmul(cross_norm, w[6]).astype(bf16)
    head_of = (jnp.arange(width)[None, :] // HD == jnp.arange(H)[:, None]).astype(bf16)
    q_heads = head_of * cross_q
    cross_scores = jnp.where(key_valid, mm_t(q_heads, cross_k) * scale, neg_fill)
    cross_probs = jax.nn.softmax(cross_scores, axis=-1)
    cross_probs_b = cross_probs.astype(bf16)
    cross_att = jnp.sum(
        matmul(cross_probs_b, cross_v) * head_of.astype(f32), axis=0, keepdims=True
    ).astype(bf16)
    dec_two = dec_one + matmul(cross_att, w[9])
    ffn_norm = rms_gain(dec_two, gain_f[5]).astype(bf16)
    pre_dec = matmul(ffn_norm, w_in_d)
    inner_dec = gelu_tanh(pre_dec).astype(bf16)
    dec_out = dec_two + matmul(inner_dec, w_out_d)

    g_top_b = cotangent.reshape(1, width)
    g_top = g_top_b.astype(f32)
    g_pre_dec = gelu_pull(pre_dec, mm_t(g_top_b, w_out_d)).astype(bf16)
    g_two_norm, g_gain_five = rms_pull(dec_two, gain_f[5], mm_t(g_pre_dec, w_in_d))
    g_two = g_top + g_two_norm
    g_two_b = g_two.astype(bf16)
    g_att = mm_t(g_two_b, w[9]).astype(bf16)
    g_att_heads = head_of * g_att
    g_probs = mm_t(g_att_heads, cross_v)
    g_cross_v = mm_outer(cross_probs_b, g_att_heads).astype(bf16)
    g_scores = cross_probs * (g_probs - jnp.sum(g_probs * cross_probs, axis=-1, keepdims=True))
    g_scores_b = g_scores.astype(bf16)
    g_cross_q = (
        jnp.sum(matmul(g_scores_b, cross_k) * head_of.astype(f32), axis=0, keepdims=True) * scale
    ).astype(bf16)
    g_cross_k = (mm_outer(g_scores_b, q_heads) * scale).astype(bf16)
    g_one_norm, g_gain_four = rms_pull(dec_one, gain_f[4], mm_t(g_cross_q, w[6]))
    g_one_b = (g_two + g_one_norm).astype(bf16)
    g_self_values = mm_t(g_one_b, w[5]).astype(bf16)
    g_gain_three = rms_pull(dec_row, gain_f[3], mm_t(g_self_values, w[4]))[1]

    lefts = (self_norm, self_values, cross_norm, cross_att, ffn_norm, inner_dec)
    rights = (g_self_values, g_one_b, g_cross_q, g_two_b, g_pre_dec, g_top_b)
    packed = lax.all_gather(jnp.concatenate(lefts + rights, axis=1), AXES, axis=0, tiled=True)
    me = (
        lax.axis_index("dp") * lax.axis_size("seq") + seq_pos
    ) * lax.axis_size("head") + lax.axis_index("head")
    devices = packed.shape[0]
    cuts = [0]
    for piece in lefts + rights:
        cuts.append(cuts[-1] + piece.shape[1])
    dec_grads = []
    for n in range(6):
        share = lefts[n].shape[1] // devices
        left = lax.dynamic_slice_in_dim(packed, cuts[n] + me * share, share, 1)
        right = packed[:, cuts[6 + n] : cuts[7 + n]]
        dec_grads.append(mm_outer(left, right))

    g_w7 = mm_outer(encoded, g_cross_k)
    g_w8 = mm_outer(encoded, g_cross_v)
    g_encoded = mm_t(g_cross_k, w[7]) + mm_t(g_cross_v, w[8])
    g_hidden_two, g_gain_two = rms_pull(hidden_two, gain_f[2], g_encoded)
    g_hidden_two_b = g_hidden_two.astype(bf16)
    g_out_e = mm_outer(inner_act, g_hidden_two_b)
    g_pre = gelu_pull(pre_act, mm_t(g_hidden_two_b, w_out_e)).astype(bf16)
    g_in_e = mm_outer(normed_two, g_pre)
    g_hidden_norm, g_gain_one = rms_pull(hidden, gain_f[1], mm_t(g_pre, w_in_e))
    g_hidden = g_hidden_two + g_hidden_norm
    g_hidden_b = g_hidden.astype(bf16)
    g_w3 = mm_outer(attended, g_hidden_b)
    g_attended = mm_t(g_hidden_b, w[3]).astype(bf16)
    gq, gk, gv, g_table = attend_bwd(length, table, q, k, v, g_attended)
    g_bias_here = jnp.einsum("ob,ho->bh", one_hot, g_table[:, 0, :], precision=highest_precision)
    g_w0 = mm_outer(normed, gq)
    g_w1 = mm_outer(normed, gk)
    g_w2 = mm_outer(normed, gv)
    g_normed = mm_t(gq, w[0]) + mm_t(gk, w[1]) + mm_t(gv, w[2])
    g_input_norm, g_gain_zero = rms_pull(x_f, gain_f[0], g_normed)
    g_x = (g_hidden + g_input_norm).astype(bf16)
    input_grad = lax.all_to_all(g_x[None], "seq", split_axis=1, concat_axis=0, tiled=True).astype(
        f32
    )

    def scatter_rows(x):
        return lax.psum_scatter(
            x.astype(bf16), AXES, scatter_dimension=x.ndim - 2, tiled=True
        ).astype(f32)

    s_78 = scatter_rows(jnp.stack((g_w7, g_w8)))
    s_out = scatter_rows(g_out_e)
    s_in = scatter_rows(g_in_e)
    s_0123 = scatter_rows(jnp.stack((g_w0, g_w1, g_w2, g_w3)))
    summed_sq = jnp.stack(
        (
            s_0123[0],
            s_0123[1],
            s_0123[2],
            s_0123[3],
            dec_grads[0],
            dec_grads[1],
            dec_grads[2],
            s_78[0],
            s_78[1],
            dec_grads[3],
        )
    )
    summed_in = jnp.stack((s_in, dec_grads[4]))
    summed_out = jnp.stack((s_out, dec_grads[5]))
    g_gains = jnp.stack(
        (g_gain_zero, g_gain_one, g_gain_two, g_gain_three, g_gain_four, g_gain_five)
    )
    g_gains, g_bias = lax.psum((g_gains, g_bias_here), AXES)
    gain_share = gains.shape[1]
    summed_gain = lax.dynamic_slice_in_dim(g_gains, me * gain_share, gain_share, 1)
    local_squares = (
        jnp.sum(summed_sq * summed_sq)
        + jnp.sum(summed_in * summed_in)
        + jnp.sum(summed_out * summed_out)
    )
    shard_squares = lax.psum(local_squares, AXES)
    grad_norm = jnp.sqrt(shard_squares + jnp.sum(g_gains * g_gains) + jnp.sum(g_bias * g_bias))
    factor = clip_bound / jnp.maximum(grad_norm, clip_bound)
    return (
        dec_out.astype(bf16).reshape(dec_in.shape),
        input_grad,
        grad_norm,
        *adam_step(square, square_m, square_v, summed_sq, factor, rate_matrix, decay_rate),
        *adam_step(ffn_in, ffn_in_m, ffn_in_v, summed_in, factor, rate_matrix, decay_rate),
        *adam_step(ffn_out, ffn_out_m, ffn_out_v, summed_out, factor, rate_matrix, decay_rate),
        *adam_step(gains, gains_m, gains_v, summed_gain, factor, rate_small, 0.0),
        *adam_step(rel_bias, rel_bias_m, rel_bias_v, g_bias, factor, rate_small, 0.0),
    )


def solution(mesh):
    rows = P(("dp", "head"), "seq", None)
    shard = P(None, AXES, None)
    small = P(None, AXES)
    return jax.shard_map(
        on_device,
        mesh=mesh,
        in_specs=(rows, rows, rows, P(("dp", "head")), P())
        + (shard,) * 9
        + (small,) * 3
        + (P(),) * 3,
        out_specs=(rows, rows, P()) + (shard,) * 9 + (small,) * 3 + (P(),) * 3,
        check_vma=False,
    )
```

time: 1470 us -> 945 us (0.64)
  local copies, waits for them, and re-layouts: 373 us -> 30.6 us
  blocking collectives: 205 us -> 131 us
  waiting for transfers between devices: 623 us -> 557 us
  matrix products: 171 us -> 107 us
  Pallas kernels: 0 us -> 52.2 us
  other arithmetic: 65.3 us -> 27.1 us
    reduce_scatter x5 -> x2, waiting for transfers between devices: 575 us -> 217 us  [scatter_rows(): lax.psum_scatter(x.astype(bf16), AXES, scatter_dimension=x.ndim - 2, tile...]
    gather x3 -> x0, local copies, waits for them, and re-layouts: 261 us -> none  [on_device(): buckets = bucket_table[offsets]]
    all_gather x5 -> x6, waiting for transfers between devices: 48 us -> 287 us  [gather_rows(): return lax.all_gather(x.astype(bf16), AXES, axis=x.ndim - 2, tiled=True)]
    unnamed x3 -> x0, blocking collectives: 72.6 us -> none
    unnamed x10 -> x12, waiting for transfers between devices: 0.16 us -> 52.9 us
    dot_general x49 -> x50, matrix products: 159 us -> 107 us  [the longest x16 42.3 us: matmul(): return jnp.dot(left, right, preferred_element_type=f32)]
    pallas_call x0 -> x2, Pallas kernels: none -> 52.2 us  [the longest x1 32.9 us: attend_bwd(): pl.pallas_call(attend_bwd_kernel, grid=(width // (2 * HD),), out_shape=(l...]
    eq x1 -> x0, local copies, waits for them, and re-layouts: 37.3 us -> none  [on_device(): buckets[None, :, :] == jnp.arange(bucket_count)[:, None, None]]
  transfers between devices with their start and end apart: 11 -> 12, of which waited for: 5 -> 9; matrix products, arithmetic and copies ran while one was open for 33% -> 13% of each run, Pallas kernels for 0% -> 6%
where the time goes in v1:
time: 945 us; the launch traced here: 939 us
  waiting for transfers between devices  557 us (59%)
  blocking collectives  131 us (14%)
  matrix products  107 us (11%)
  Pallas kernels  52.2 us (6%)
  local copies, waits for them, and re-layouts  30.6 us (3%)
  other arithmetic  27.1 us (3%)
  between operations  24.2 us (3%)
  starting transfers between devices  9.5 us (1%)
    all_gather x6, waiting for transfers between devices, gather_rows(): return lax.all_gather(x.astype(bf16), AXES, axis=x.ndim - 2, tiled=True)  287 us
    reduce_scatter x2, waiting for transfers between devices, scatter_rows(): lax.psum_scatter(x.astype(bf16), AXES, scatter_dimension=x.ndim - 2, tile...  217 us
    unnamed x12, waiting for transfers between devices  52.9 us
    all_gather x1, blocking collectives, on_device(): lax.all_gather(jnp.concatenate(lefts + rights, axis=1), AXES, axis=0, til...  47.1 us
    all_gather x1, blocking collectives, on_device(): lax.all_gather(gains.astype(bf16), AXES, axis=1, tiled=True).astype(f32)  43.9 us
    dot_general x16, matrix products, matmul(): return jnp.dot(left, right, preferred_element_type=f32)  42.3 us
    psum x1, blocking collectives, on_device(): shard_squares = lax.psum(local_squares, AXES)  40.5 us
    dot_general x16, matrix products, mm_t(): lax.dot_general(left, right, (((1,), (1,)), ((), ())), preferred_element_...  37.1 us
  transfers between devices with their start and end apart: 12, of which 9 were waited for; matrix products, arithmetic and copies ran while one was open for 13% of the time, Pallas kernels for 6%

profile of v1, /device:TPU:0, one launch (start us, length us, event | category | flops | bytes accessed | tf_op | source)
XLA Modules:
  0.0 938.8 jit_solution(14363541747341977469)
XLA Ops:
  7.3 1.2 convert.46
  12.9 5.2 all-to-all-start
  19.4 43.9 %all-gather.4 = bf16[32,24,6]{1,2,0:T(8,128)(2,1)S(1)} all-gather(bf16[1,24,6]{1,2,0:T(8,128)(2,1)S(1)} %convert_bitcast_fusion), channel_id=1, replica_groups=mesh['dp'=4,'seq'=4,'head'=2] {'dp','seq','head'}, dimensions={0}, use_global_device_ids=true | all-gather | bytes 9504 | tf_op jit(solution)/shard_map/all_gather | solution.py:245
  66.0 15.1 %all-gather.15.cloned.1.call-done = bf16[4,768,768]{2,1,0:T(8,128)(2,1)} async-done(((bf16[4,24,768]{2,1,0:T(8,128)(2,1)}), bf16[4,768,768]{2,1,0:T(8,128)(2,1)}) %all-gather.15.cloned.1.call-update) | async-done | bytes 4718608 | tf_op jit(solution)/shard_map/all_gather | solution.py:237
  81.1 2.2 convolution_convert_fusion.12.v_ref
  83.3 2.0 convolution_convert_fusion.13.k_ref
  85.4 1.9 convolution_convert_fusion.14.q_ref
  87.3 19.3 %attend_fwd.1 = bf16[512,768]{1,0:T(8,128)(2,1)S(1)} custom-call(s32[1]{0:T(128)} %dynamic_slice.24.len_ref, f32[12,1,1024]{2,1,0:T(1,128)S(1)} %broadcast_in_dim.31.table_ref, bf16[512,768]{1,0:T(8,128)(2,1)S(1)} %convolution_convert_fusion.14.q_ref, bf16[512,768]{1,0:T(8,128)(2,1)S(1)} %convolution_convert_fusion.13.k_ref, ...), custom_call_target="tpu_custom_call" | custom-call | tf_op jit(solution)/shard_map/attend_fwd/pallas_call | solution.py:178
  106.6 1.9 multiply_reduce_fusion.5
  108.6 38.6 %all-gather.17.cloned.1.call-done = bf16[1,768,3072]{2,1,0:T(8,128)(2,1)} async-done(((bf16[1,24,3072]{2,1,0:T(8,128)(2,1)}), bf16[1,768,3072]{2,1,0:T(8,128)(2,1)}) %all-gather.17.cloned.1.call-update) | async-done | bytes 4718608 | tf_op jit(solution)/shard_map/all_gather | solution.py:237
  147.2 8.1 fusion.21
  155.3 57.8 %all-gather.19.cloned.1.call-done = bf16[1,3072,768]{2,1,0:T(8,128)(2,1)} async-done(((bf16[1,96,768]{2,1,0:T(8,128)(2,1)}), bf16[1,3072,768]{2,1,0:T(8,128)(2,1)}) %all-gather.19.cloned.1.call-update) | async-done | bytes 4718608 | tf_op jit(solution)/shard_map/all_gather | solution.py:237
  213.1 8.5 multiply_reduce_fusion.4
  221.6 1.2 copy-done.4
  222.8 1.1 multiply_convert_fusion.2
  223.9 55.1 %all-gather.23.cloned.1.call-done = bf16[1,3072,768]{2,1,0:T(8,128)(2,1)} async-done(((bf16[1,96,768]{2,1,0:T(8,128)(2,1)}), bf16[1,3072,768]{2,1,0:T(8,128)(2,1)}) %all-gather.23.cloned.1.call-update) | async-done | bytes 4718608 | tf_op jit(solution)/shard_map/all_gather | solution.py:237
  278.9 3.6 fusion.7
  282.6 71.1 %all-gather.13.cloned.1.call-done = bf16[6,768,768]{2,1,0:T(8,128)(2,1)} async-done(((bf16[6,24,768]{2,1,0:T(8,128)(2,1)}), bf16[6,768,768]{2,1,0:T(8,128)(2,1)}) %all-gather.13.cloned.1.call-update) | async-done | bytes 7077904 | tf_op jit(solution)/shard_map/all_gather | solution.py:237
  353.6 1.6 convolution_reduce_fusion.6
  355.2 1.6 convolution_reduce_fusion.5
  358.1 1.6 convolution_reduce_fusion.4
  359.7 2.4 convolution_convert_fusion.11
  363.1 2.1 convolution_convert_fusion.10
  366.4 1.6 convolution_reduce_fusion.3
  369.3 49.7 %all-gather.21.cloned.1.call-done = bf16[1,768,3072]{2,1,0:T(8,128)(2,1)} async-done(((bf16[1,24,3072]{2,1,0:T(8,128)(2,1)}), bf16[1,768,3072]{2,1,0:T(8,128)(2,1)}) %all-gather.21.cloned.1.call-update) | async-done | bytes 4718608 | tf_op jit(solution)/shard_map/all_gather | solution.py:237
  419.1 3.2 fusion.13
  422.8 1.9 fusion.142
  425.4 3.1 fusion.52
  428.6 1.8 convolution_reduce_fusion.2
  434.9 2.4 copy.66
  437.3 1.9 copy.78
  439.3 2.5 fusion.58
  441.8 2.8 multiply_reduce_fusion
  445.0 8.8 fusion.6
  453.9 2.9 multiply_reduce_fusion.1
  458.1 32.9 %attend_bwd.1 = (bf16[512,768]{1,0:T(8,128)(2,1)S(1)}, bf16[512,768]{1,0:T(8,128)(2,1)S(1)}, bf16[512,768]{1,0:T(8,128)(2,1)S(1)}, f32[12,1,1024]{2,1,0:T(1,128)S(1)}) custom-call(s32[1]{0:T(128)} %dynamic_slice.24.len_ref, f32[12,1,1024]{2,1,0:T(1,128)S(1)} %broadcast_in_dim.31.table_ref, bf16[512,768]{1,0:T(8,128)(2,1)S(1)} %convolution_convert_fusion.14.q_ref, ...), custom_call_target="tpu_custom_call" | custom-call | tf_op jit(solution)/shard_map/attend_bwd/pallas_call | solution.py:196
  491.8 2.2 fusion.57
  494.0 2.4 fusion.31
  500.9 3.6 copy.64
  504.6 3.2 copy.77
  508.0 1.1 copy-done.7
  509.1 8.3 convolution_convert_fusion
  517.6 1.0 copy-done.18
  519.1 6.3 convolution_convert_fusion.1
  525.5 2.3 fusion.143
  528.6 1.7 convolution_reduce_fusion.1
  530.3 1.2 copy.90
  532.1 5.4 reduce.40
  537.5 1.0 reshape.509
  538.5 3.7 all-to-all-start.1
  542.4 1.7 convolution_reduce_fusion
  544.2 47.1 %all-gather.5 = bf16[32,1,13824]{2,1,0:T(2,128)(2,1)S(1)} all-gather(bf16[1,1,13824]{2,1,0:T(2,128)(2,1)S(1)} %bitcast.302), channel_id=1, replica_groups=mesh['dp'=4,'seq'=4,'head'=2] {'dp','seq','head'}, dimensions={0}, use_global_device_ids=true | all-gather | bytes 912384 | tf_op jit(solution)/shard_map/all_gather | solution.py:322
  591.5 1.0 copy.89
  593.7 1.0 convolution_bitcast_fusion.1
  594.7 1.1 convolution_bitcast_fusion
  597.9 51.7 %reduce-scatter.13.cloned.1.call-done = bf16[24,3072]{1,0:T(8,128)(2,1)} async-done(((bf16[768,3072]{1,0:T(8,128)(2,1)}), bf16[24,3072]{1,0:T(8,128)(2,1)}) %reduce-scatter.13.cloned.1.call-update) | async-done | bytes 147472
  649.7 1.0 reshape.492
  650.7 110.6 %reduce-scatter.11.cloned.1.call-done = bf16[96,768]{1,0:T(8,128)(2,1)} async-done(((bf16[3072,768]{1,0:T(8,128)(2,1)}), bf16[96,768]{1,0:T(8,128)(2,1)}) %reduce-scatter.11.cloned.1.call-update) | async-done | bytes 147472 | tf_op jit(solution)/shard_map/reduce_scatter | solution.py:363
  767.5 106.1 %reduce-scatter.9.cloned.1.call-done = bf16[24,3072]{1,0:T(8,128)(2,1)} async-done(((bf16[768,3072]{1,0:T(8,128)(2,1)}), bf16[24,3072]{1,0:T(8,128)(2,1)}) %reduce-scatter.9.cloned.1.call-update) | async-done | bytes 147472 | tf_op jit(solution)/shard_map/reduce_scatter | solution.py:363
  877.2 1.2 copy.68
  878.4 40.5 %all-reduce.1 = (f32[]{:T(128)}, f32[6,768]{1,0:T(8,128)S(1)}, f32[32,12]{0,1:T(8,128)S(1)}) all-reduce(f32[]{:T(128)S(6)} %add.307, f32[6,768]{1,0:T(8,128)S(1)} %stack.108, f32[32,12]{0,1:T(8,128)S(1)} %fusion.62), channel_id=1, replica_groups=mesh['dp'=4,'seq'=4,'head'=2] {'dp','seq','head'}, use_global_device_ids=true, to_apply=%region_23.24 | all-reduce | flops 4993 | bytes 39944 | tf_op jit(solution)/shard_map/psum | solution.py:398
  922.8 3.0 multiply_subtract_fusion.1
  925.9 1.5 multiply_subtract_fusion.2
  928.1 1.8 multiply_subtract_fusion
  (227 shorter events, 39.0 us)
Async XLA Ops:
  7.2 2.1 copy-start.15
  7.2 2.9 copy-start.14
  7.2 73.9 %all-gather.15.cloned.1.call-start = ((), (), s32[]{:S(2)}) async-start(), calls=%async_computation.7 | async-start | bytes 4866048 | tf_op jit(solution)/shard_map/all_gather | solution.py:237
  9.2 138.0 %all-gather.17.cloned.1.call-start = ((), (), s32[]{:S(2)}) async-start(), calls=%async_computation.10 | async-start | bytes 4866048 | tf_op jit(solution)/shard_map/all_gather | solution.py:237
  10.1 203.1 %all-gather.19.cloned.1.call-start = ((), (), s32[]{:S(2)}) async-start(), calls=%async_computation.11 | async-start | bytes 4866048 | tf_op jit(solution)/shard_map/all_gather | solution.py:237
  10.9 7.2 copy-start.30
  10.9 7.2 copy-start.28
  10.9 268.0 %all-gather.23.cloned.1.call-start = ((), (), s32[]{:S(2)}) async-start(), calls=%async_computation.13 | async-start | bytes 4866048 | tf_op jit(solution)/shard_map/all_gather | solution.py:237
  11.5 342.2 %all-gather.13.cloned.1.call-start = ((), (), s32[]{:S(2)}) async-start(), calls=%async_computation.6 | async-start | bytes 7299072 | tf_op jit(solution)/shard_map/all_gather | solution.py:237
  11.6 52.0 %copy-start.34 = (s32[1023]{0:T(1024)S(1)}, s32[1023]{0:T(1024)}, u32[]{:S(2)}) copy-start(s32[1023]{0:T(1024)} %param.24) | copy-start | bytes 12280
  11.6 52.1 %copy-start.31 = (f32[32,12]{0,1:T(8,128)S(1)}, f32[32,12]{0,1:T(8,128)}, u32[]{:S(2)}) copy-start(f32[32,12]{0,1:T(8,128)} %param.37) | copy-start | bytes 4612
  11.6 52.5 %copy-start.37 = (s32[4]{0:T(128)S(1)}, s32[4]{0:T(128)}, u32[]{:S(2)}) copy-start(s32[4]{0:T(128)} %param.23) | copy-start | bytes 52
  12.4 406.7 %all-gather.21.cloned.1.call-start = ((), (), s32[]{:S(2)}) async-start(), calls=%async_computation.12 | async-start | bytes 4866048 | tf_op jit(solution)/shard_map/all_gather | solution.py:237
  12.9 52.5 %all-to-all-start = ((bf16[4,128,768]{2,1,0:T(8,128)(2,1)}), bf16[4,128,768]{2,1,0:T(8,128)(2,1)S(1)}, u32[]{:S(2)}, u32[]{:S(2)}) async-start(bf16[4,128,768]{2,1,0:T(8,128)(2,1)} %param.20), calls=%async_computation | async-start | bytes 1572864 | tf_op jit(solution)/shard_map/all_to_all | solution.py:255
  18.1 578.9 %reduce-scatter.15.cloned.1.call-start = ((), (), s32[]{:S(2)}) async-start(), calls=%async_computation.15 | async-start | bytes 2433024
  65.5 17.9 %copy-start = (bf16[4,128,768]{2,1,0:T(8,128)(2,1)}, bf16[4,128,768]{2,1,0:T(8,128)(2,1)S(1)}, u32[]{:S(2)}) copy-start(bf16[4,128,768]{2,1,0:T(8,128)(2,1)S(1)} %all-to-all-done) | copy-start | bytes 2359300
  66.0 17.4 %copy-start.20 = (bf16[4,128,768]{2,1,0:T(8,128)(2,1)}, bf16[4,128,768]{2,1,0:T(8,128)(2,1)S(1)}, u32[]{:S(2)}) copy-start(bf16[4,128,768]{2,1,0:T(8,128)(2,1)S(1)} %fusion.34) | copy-start | bytes 2359300
  81.1 4.3 copy-start.27
  87.3 19.3 %copy-start.1 = (bf16[4,128,768]{2,1,0:T(8,128)(2,1)S(1)}, bf16[4,128,768]{2,1,0:T(8,128)(2,1)}, u32[]{:S(2)}) copy-start(bf16[4,128,768]{2,1,0:T(8,128)(2,1)} %copy-done) | copy-start | bytes 2359300
  221.6 1.2 copy-start.4
  221.6 57.4 %copy-start.29 = (bf16[1,1,768]{2,1,0:T(2,128)(2,1)S(1)}, bf16[1,1,768]{2,1,0:T(2,128)(2,1)}, u32[]{:S(2)}) copy-start(bf16[1,1,768]{2,1,0:T(2,128)(2,1)} %param.22) | copy-start | bytes 4612
  359.7 3.5 copy-start.21
  362.0 0.9 copy-start.17
  365.2 0.9 copy-start.10
  419.1 3.8 copy-start.3
  425.4 5.0 copy-start.11
  428.6 3.0 copy-start.22
  431.6 0.9 copy-start.12
  433.0 0.9 copy-start.19
  439.2 210.4 %reduce-scatter.13.cloned.1.call-start = ((), (), s32[]{:S(2)}) async-start(), calls=%async_computation.14 | async-start | bytes 4866048
  439.3 2.5 copy-start.5
  439.3 5.6 slice-start
  441.8 3.2 slice-start.1
  444.6 9.3 slice-start.2
  444.6 12.6 %slice-start.4 = ((s8[4718592]{0:T(1024)(128)(4,1)}), s8[4194304]{0:T(1024)(128)(4,1)S(1)}, s32[]{:S(2)}) async-start(s8[4718592]{0:T(1024)(128)(4,1)} %bitcast.300), calls=%async_computation.20 | async-start | bytes 8388608
  445.0 11.8 %copy-start.6 = (f32[512,768]{1,0:T(8,128)}, f32[512,768]{1,0:T(8,128)S(1)}, u32[]{:S(2)}) copy-start(f32[512,768]{1,0:T(8,128)S(1)} %add_add_fusion.2) | copy-start | bytes 4718596
  445.0 8.9 copy-start.8
  445.0 8.9 slice-start.3
  445.0 12.2 %slice-start.5 = ((s8[4718592]{0:T(1024)(128)(4,1)}), s8[524288]{0:T(1024)(128)(4,1)S(1)}, s32[]{:S(2)}) async-start(s8[4718592]{0:T(1024)(128)(4,1)} %bitcast.300), calls=%async_computation.21 | async-start | bytes 1048576
  453.9 2.9 copy-start.38
  491.8 2.2 copy-start.2
  507.7 1.4 copy-start.7
  507.8 253.5 %reduce-scatter.11.cloned.1.call-start = ((), (), s32[]{:S(2)}) async-start(), calls=%async_computation.9 | async-start | bytes 4866048 | tf_op jit(solution)/shard_map/reduce_scatter | solution.py:363
  517.5 1.1 copy-start.18
  517.5 1.7 copy-start.9
  517.5 356.0 %reduce-scatter.9.cloned.1.call-start = ((), (), s32[]{:S(2)}) async-start(), calls=%async_computation.8 | async-start | bytes 4866048 | tf_op jit(solution)/shard_map/reduce_scatter | solution.py:363
  538.5 57.7 %all-to-all-start.1 = ((bf16[4,2,49152]{2,1,0:T(2,128)(2,1)}), bf16[4,2,49152]{2,1,0:T(2,128)(2,1)S(1)}, u32[]{:S(2)}, u32[]{:S(2)}) async-start(bf16[4,2,49152]{2,1,0:T(2,128)(2,1)} %reshape.509), calls=%async_computation.1 | async-start | bytes 1572864 | tf_op jit(solution)/shard_map/all_to_all | solution.py:358
  877.2 45.0 %copy-start.32 = (f32[32,12]{0,1:T(8,128)S(1)}, f32[32,12]{0,1:T(8,128)}, u32[]{:S(2)}) copy-start(f32[32,12]{0,1:T(8,128)} %param.38) | copy-start | bytes 4612
  877.2 45.0 %copy-start.33 = (f32[32,12]{0,1:T(8,128)S(1)}, f32[32,12]{0,1:T(8,128)}, u32[]{:S(2)}) copy-start(f32[32,12]{0,1:T(8,128)} %param.39) | copy-start | bytes 4612
  922.8 3.0 copy-start.16
  922.8 3.0 copy-start.25
  922.8 3.0 copy-start.26
  925.9 1.6 copy-start.13
  925.9 1.8 copy-start.23
  925.9 2.2 copy-start.24
  928.1 1.8 copy-start.35
  928.1 1.8 copy-start.36
Sparse Core Ops, SparseCore 0:
  11.6 69.5 all-gather.14
  84.6 62.5 all-gather.16
  150.6 62.4 all-gather.18
  216.5 62.4 all-gather.22
  282.3 71.2 all-gather.12
  357.0 62.0 all-gather.20
  439.3 97.8 reduce-scatter.14
  543.6 105.9 reduce-scatter.12
  655.1 106.0 reduce-scatter.10
  767.4 106.0 reduce-scatter.8

commit v2 on v1

--- a/solution.py
+++ b/solution.py
@@ -211,6 +211,527 @@
     )(length, table, q, k, v, do)
 
 
+MESH_ID = pl.DeviceIdType.MESH
+HALF = 384
+ROWS = 48
+MIB = 1024 * 1024
+
+
+def place():
+    z, s, c = lax.axis_index("dp"), lax.axis_index("seq"), lax.axis_index("head")
+    near = s + 1 - 2 * (s % 2)
+    far = (s + 2) % 4
+    first = near + c * (far - near)
+    second = far + c * (near - far)
+    return z, s, c, first, second, 3 - s
+
+
+def greet(z, s, c, z_count):
+    barrier = pltpu.get_barrier_semaphore()
+    for d in range(1, z_count):
+        peer = ((z + d) % z_count, s, c)
+        pl.semaphore_signal(barrier, 1, device_id=peer, device_id_type=MESH_ID)
+    for d in range(1, 4):
+        peer = (z, (s + d) % 4, c)
+        pl.semaphore_signal(barrier, 1, device_id=peer, device_id_type=MESH_ID)
+    pl.semaphore_signal(barrier, 1, device_id=(z, s, 1 - c), device_id_type=MESH_ID)
+    pl.semaphore_wait(barrier, z_count + 3)
+
+
+def remote(src, dst, send, recv, peer):
+    return pltpu.make_async_remote_copy(
+        src, dst, send, recv, device_id=peer, device_id_type=MESH_ID
+    )
+
+
+def cols(c, base=0):
+    return pl.ds(pl.multiple_of(base + c * HALF, 128), HALF)
+
+
+def unit_view(kind, n, ref, z, s, c):
+    if kind == "square":
+        return ref.at[n, z, s, :, cols(c)]
+    if kind == "cols":
+        return ref.at[n // 4, z, s, :, cols(c, (n % 4) * 2 * HALF)]
+    if kind == "rows":
+        return ref.at[n // 4, z, s, pl.ds((n % 4) * ROWS, ROWS), cols(c)]
+    return ref.at[z, s]
+
+
+class Gather:
+    def __init__(self, units, refs, send, recv, z_count):
+        self.units, self.refs, self.send, self.recv = units, refs, send, recv
+        self.z_count = z_count
+        self.where = place()
+        self.started = []
+
+    def view(self, u, z, s, c):
+        kind, n = self.units[u]
+        return unit_view(kind, n, self.refs[kind], z, s, c)
+
+    def go(self, u, slot, ref, peer):
+        copy = remote(ref, ref, self.send.at[u, slot], self.recv.at[u, slot], peer)
+        copy.start()
+        self.started.append(copy)
+
+    def got(self, u, slot, ref):
+        z, s, c = self.where[:3]
+        remote(ref, ref, self.send.at[u, slot], self.recv.at[u, slot], (z, s, 1 - c)).wait_recv()
+
+    def z_start(self, u):
+        z, s, c = self.where[:3]
+        for d in range(1, self.z_count):
+            self.go(u, d - 1, self.view(u, z, s, c), ((z + d) % self.z_count, s, c))
+
+    def z_wait(self, u):
+        z, s, c = self.where[:3]
+        for d in range(1, self.z_count):
+            self.got(u, d - 1, self.view(u, (z + self.z_count - d) % self.z_count, s, c))
+
+    def a_start(self, u):
+        z, s, c, first, second, both = self.where
+        self.go(u, 3, self.view(u, slice(None), s, c), (z, first, c))
+
+    def a_wait(self, u):
+        z, s, c, first, second, both = self.where
+        self.got(u, 3, self.view(u, slice(None), first, c))
+
+    def b_start(self, u):
+        z, s, c, first, second, both = self.where
+        self.go(u, 4, self.view(u, slice(None), s, c), (z, second, c))
+        self.go(u, 5, self.view(u, slice(None), first, c), (z, second, c))
+
+    def b_wait(self, u):
+        z, s, c, first, second, both = self.where
+        self.got(u, 4, self.view(u, slice(None), second, c))
+        self.got(u, 5, self.view(u, slice(None), both, c))
+
+    def s_start(self, u):
+        z, s, c = self.where[:3]
+        if self.units[u][0] != "gain":
+            self.go(u, 6, self.view(u, slice(None), slice(None), c), (z, s, 1 - c))
+
+    def s_wait(self, u):
+        z, s, c = self.where[:3]
+        if self.units[u][0] != "gain":
+            self.got(u, 6, self.view(u, slice(None), slice(None), 1 - c))
+
+    def tick(self, t, skew=2, done=None):
+        steps = (
+            (self.z_start,),
+            (self.z_wait, self.a_start),
+            (self.a_wait, self.b_start),
+            (self.b_wait, self.s_start),
+            (self.s_wait,) + ((done,) if done else ()),
+        )
+        for n, work in enumerate(steps):
+            u = t - n * skew
+            if 0 <= u < len(self.units):
+                for step in work:
+                    step(u)
+
+    def finish(self):
+        for copy in self.started:
+            copy.wait_send()
+
+
+def gather_kernel(
+    units, z_count, sq_ref, in_ref, out_ref, gain_ref, x_ref,
+    sq_o, in_o, out_o, gain_o, x_o,
+    sq_w, in_w, out_w, gain_w, sq_r, in_r, out_r, gain_r,
+    send, recv, first_send, first_recv, x_send, x_recv, local,
+):
+    z, s, c = place()[:3]
+    sibling = (z, s, 1 - c)
+    n_sq, n_ff = sq_ref.shape[0], in_ref.shape[0]
+    greet(z, s, c, z_count)
+
+    first = []
+
+    def to_sibling(src, dst):
+        copy = remote(src, dst, first_send.at[len(first)], first_recv.at[len(first)], sibling)
+        copy.start()
+        first.append(copy)
+
+    to_sibling(gain_ref, gain_r)
+    to_sibling(sq_ref.at[:, :, cols(1 - c)], sq_r)
+    for n in range(n_ff):
+        for j in range(4):
+            to_sibling(in_ref.at[n, :, cols(1 - c, 2 * HALF * j)], in_r.at[n, j])
+        to_sibling(out_ref.at[n, :, cols(1 - c)], out_r.at[n])
+    x_copies = []
+    for d in range(1, 4):
+        peer = (s + d) % 4
+        copy = remote(
+            x_ref.at[peer], x_o.at[s], x_send.at[d - 1], x_recv.at[d - 1], (z, peer, c)
+        )
+        copy.start()
+        x_copies.append(copy)
+    mine = pltpu.make_async_copy(x_ref.at[s], x_o.at[s], local.at[0])
+    mine.start()
+
+    def joined(own, other):
+        top = jnp.where(c == 0, own, other)
+        bottom = jnp.where(c == 0, other, own)
+        return jnp.concatenate([top, bottom], axis=0).astype(bf16)
+
+    first[0].wait_recv()
+    gain_w[z, s] = joined(gain_ref[...], gain_r[...])
+    first[1].wait_recv()
+    for n in range(n_sq):
+        sq_w[n, z, s, :, cols(c)] = joined(sq_ref[n, :, cols(c)], sq_r[n])
+    k = 2
+    for n in range(n_ff):
+        for j in range(4):
+            first[k].wait_recv()
+            k += 1
+            at = cols(c, 2 * HALF * j)
+            in_w[n, z, s, :, at] = joined(in_ref[n, :, at], in_r[n, j])
+        first[k].wait_recv()
+        k += 1
+        out_w[n, z, s, :, cols(c)] = joined(out_ref[n, :, cols(c)], out_r[n])
+
+    gather = Gather(
+        units,
+        {"square": sq_w, "cols": in_w, "rows": out_w, "gain": gain_w},
+        send,
+        recv,
+        z_count,
+    )
+    outs = {"square": sq_o, "cols": in_o, "rows": out_o, "gain": gain_o}
+    drains = []
+
+    def done(u):
+        kind, n = units[u]
+        if kind == "square":
+            src, dst = sq_w.at[n], sq_o.at[n]
+        elif kind == "gain":
+            src, dst = gain_w, gain_o
+        elif n % 4 != 3:
+            return
+        elif kind == "cols":
+            src, dst = in_w.at[n // 4], in_o.at[n // 4]
+        else:
+            src, dst = out_w.at[n // 4], out_o.at[n // 4]
+        copy = pltpu.make_async_copy(src, dst, local.at[1 + len(drains)])
+        copy.start()
+        drains.append(copy)
+
+    del outs
+    skew = 2
+    for t in range(len(units) + 4 * skew):
+        gather.tick(t, skew, done)
+    gather.finish()
+    for copy in first:
+        copy.wait_send()
+    for copy in x_copies:
+        copy.wait()
+    mine.wait()
+    for copy in drains:
+        copy.wait()
+
+
+def gather_weights(square, ffn_in, ffn_out, gains_t, x, z_count):
+    n_sq, n_ff = square.shape[0], ffn_in.shape[0]
+    order = [("gain", 0)]
+    order += [("square", n) for n in (0, 1, 2, 3)]
+    order += [("cols", n) for n in range(4)] + [("rows", n) for n in range(4)]
+    order += [("square", n) for n in (7, 8, 4, 5, 6, 9)]
+    order += [("cols", n) for n in range(4, 8)] + [("rows", n) for n in range(4, 8)]
+    sq_s = (n_sq, z_count, 4, ROWS, 2 * HALF)
+    in_s = (n_ff, z_count, 4, ROWS, 8 * HALF)
+    out_s = (n_ff, z_count, 4, 4 * ROWS, 2 * HALF)
+    gain_s = (z_count, 4, ROWS, 128)
+    firsts = 2 + 5 * n_ff
+    vmem = pl.BlockSpec(memory_space=pltpu.VMEM)
+    hbm = pl.BlockSpec(memory_space=pltpu.HBM)
+    return pl.pallas_call(
+        functools.partial(gather_kernel, order, z_count),
+        out_shape=[jax.ShapeDtypeStruct(shape, bf16) for shape in (sq_s, in_s, out_s, gain_s)]
+        + [jax.ShapeDtypeStruct(x.shape, bf16)],
+        in_specs=[vmem] * 4 + [hbm],
+        out_specs=[hbm] * 5,
+        scratch_shapes=[
+            pltpu.VMEM(sq_s, bf16),
+            pltpu.VMEM(in_s, bf16),
+            pltpu.VMEM(out_s, bf16),
+            pltpu.VMEM(gain_s, bf16),
+            pltpu.VMEM((n_sq, ROWS // 2, HALF), f32),
+            pltpu.VMEM((n_ff, 4, ROWS // 2, HALF), f32),
+            pltpu.VMEM((n_ff, 2 * ROWS, HALF), f32),
+            pltpu.VMEM((ROWS // 2, 128), f32),
+            pltpu.SemaphoreType.DMA((len(order), 7)),
+            pltpu.SemaphoreType.DMA((len(order), 7)),
+            pltpu.SemaphoreType.DMA((firsts,)),
+            pltpu.SemaphoreType.DMA((firsts,)),
+            pltpu.SemaphoreType.DMA((3,)),
+            pltpu.SemaphoreType.DMA((3,)),
+            pltpu.SemaphoreType.DMA((20,)),
+        ],
+        compiler_params=pltpu.CompilerParams(
+            collective_id=0, has_side_effects=True, vmem_limit_bytes=60 * MIB
+        ),
+        name="gather_weights",
+    )(square, ffn_in, ffn_out, gains_t, x)
+
+
+class Scatter:
+    def __init__(self, units, refs, bufs, sems, z_count):
+        self.units, self.refs, self.z_count = units, refs, z_count
+        self.r0, self.own, self.r1, self.r2, self.r3, self.fin, self.sib = bufs
+        self.send, self.recv, self.local = sems
+        self.where = place()
+        self.started = []
+        self.loads = {}
+
+    def go(self, u, slot, src, dst, peer):
+        copy = remote(src, dst, self.send.at[u, slot], self.recv.at[u, slot], peer)
+        copy.start()
+        self.started.append(copy)
+
+    def got(self, u, slot, ref):
+        z, s, c = self.where[:3]
+        remote(ref, ref, self.send.at[u, slot], self.recv.at[u, slot], (z, s, 1 - c)).wait_recv()
+
+    def view(self, u, c):
+        kind, n = self.units[u]
+        return unit_view(kind, n, self.refs[kind], slice(None), slice(None), c)
+
+    def c_start(self, u):
+        z, s, c = self.where[:3]
+        self.go(u, 0, self.view(u, 1 - c), self.r0.at[u], (z, s, 1 - c))
+        copy = pltpu.make_async_copy(self.view(u, c), self.own.at[u % 4], self.local.at[u])
+        copy.start()
+        self.loads[u] = copy
+
+    def b_start(self, u):
+        z, s, c, first, second, both = self.where
+        self.loads[u].wait()
+        self.got(u, 0, self.r0.at[u])
+        for n in range(self.z_count):
+            for m in range(4):
+                total = self.own[u % 4, n, m].astype(f32) + self.r0[u, n, m].astype(f32)
+                self.r0[u, n, m] = total.astype(bf16)
+        self.go(u, 1, self.r0.at[u, :, second], self.r1.at[u, 0], (z, second, c))
+        self.go(u, 2, self.r0.at[u, :, both], self.r1.at[u, 1], (z, second, c))
+
+    def a_start(self, u):
+        z, s, c, first, second, both = self.where
+        self.got(u, 2, self.r1.at[u, 1])
+        for n in range(self.z_count):
+            total = self.r0[u, n, first].astype(f32) + self.r1[u, 1, n].astype(f32)
+            self.r1[u, 1, n] = total.astype(bf16)
+        self.go(u, 3, self.r1.at[u, 1], self.r2.at[u], (z, first, c))
+        self.got(u, 1, self.r1.at[u, 0])
+        for n in range(self.z_count):
+            total = self.r0[u, n, s].astype(f32) + self.r1[u, 0, n].astype(f32)
+            self.r1[u, 0, n] = total.astype(bf16)
+
+    def z_start(self, u):
+        z, s, c = self.where[:3]
+        self.got(u, 3, self.r2.at[u])
+        for n in range(self.z_count):
+            total = self.r1[u, 0, n].astype(f32) + self.r2[u, n].astype(f32)
+            self.r2[u, n] = total.astype(bf16)
+        for d in range(1, self.z_count):
+            to = (z + d) % self.z_count
+            self.go(u, 3 + d, self.r2.at[u, to], self.r3.at[u, d - 1], (to, s, c))
+
+    def f_start(self, u):
+        z, s, c = self.where[:3]
+        total = self.r2[u, z].astype(f32)
+        for d in range(1, self.z_count):
+            self.got(u, 3 + d, self.r3.at[u, d - 1])
+            total = total + self.r3[u, d - 1].astype(f32)
+        self.fin[u] = total
+        kind, n = self.units[u]
+        if kind == "rows":
+            if n % 2 == 1:
+                @pl.when(c != n // 2)
+                def _():
+                    remote(
+                        self.fin.at[pl.ds(u - 1, 2)],
+                        self.sib.at[pl.ds(u - 1, 2)],
+                        self.send.at[u, 7],
+                        self.recv.at[u, 7],
+                        (z, s, 1 - c),
+                    ).start()
+        else:
+            rows = pl.ds(pl.multiple_of((1 - c) * (ROWS // 2), 8), ROWS // 2)
+            self.go(
+                u, 7, self.fin.at[u, rows], self.sib.at[u, pl.ds(0, ROWS // 2)], (z, s, 1 - c)
+            )
+
+    def finish_unit(self, u, put):
+        z, s, c = self.where[:3]
+        kind, n = self.units[u]
+        if kind == "rows":
+            if n % 2 == 1:
+
+                @pl.when(c == n // 2)
+                def _():
+                    pair = self.sib.at[pl.ds(u - 1, 2)]
+                    self.got(u, 7, pair)
+                    for k in range(2):
+                        put(kind, (n % 2 - 1 + k) * ROWS, c, self.fin[u - 1 + k])
+                        put(kind, (n % 2 - 1 + k) * ROWS, 1 - c, self.sib[u - 1 + k])
+
+                @pl.when(c != n // 2)
+                def _():
+                    pair = self.fin.at[pl.ds(u - 1, 2)]
+                    remote(
+                        pair, pair, self.send.at[u, 7], self.recv.at[u, 7], (z, s, 1 - c)
+                    ).wait_send()
+        else:
+            self.got(u, 7, self.sib.at[u, pl.ds(0, ROWS // 2)])
+            rows = pl.ds(pl.multiple_of(c * (ROWS // 2), 8), ROWS // 2)
+            put(kind, n, c, self.fin[u, rows])
+            put(kind, n, 1 - c, self.sib[u, : ROWS // 2])
+
+    def tick(self, t, put, skew=1):
+        steps = (self.c_start, self.b_start, self.a_start, self.z_start, self.f_start)
+        last = t - 5 * skew
+        if 0 <= last < len(self.units):
+            self.finish_unit(last, put)
+        for n in reversed(range(5)):
+            u = t - n * skew
+            if 0 <= u < len(self.units):
+                steps[n](u)
+
+    def finish(self):
+        for copy in self.started:
+            copy.wait_send()
+
+
+def scatter_kernel(
+    units, z_count, sq_ref, in_ref, out_ref, x_ref, sq_o, in_o, out_o, x_o,
+    r0, own, r1, r2, r3, fin, sib, send, recv, local, x_send, x_recv, x_local,
+):
+    z, s, c = place()[:3]
+    greet(z, s, c, z_count)
+    scatter = Scatter(
+        units,
+        {"square": sq_ref, "cols": in_ref, "rows": out_ref},
+        (r0, own, r1, r2, r3, fin, sib),
+        (send, recv, local),
+        z_count,
+    )
+
+    def put(kind, n, side, value):
+        if kind == "square":
+            sq_o[n, :, cols(side)] = value
+        elif kind == "cols":
+            in_o[:, cols(side, n * 2 * HALF)] = value
+        else:
+            out_o[n : n + ROWS, cols(side)] = value
+
+    x_copies = []
+    for d in range(1, 4):
+        peer = (s + d) % 4
+        copy = remote(
+            x_ref.at[peer], x_o.at[s], x_send.at[d - 1], x_recv.at[d - 1], (z, peer, c)
+        )
+        copy.start()
+        x_copies.append(copy)
+    mine = pltpu.make_async_copy(x_ref.at[s], x_o.at[s], x_local.at[0])
+    mine.start()
+    skew = 1
+    for t in range(len(units) + 5 * skew):
+        scatter.tick(t, put, skew)
+    scatter.finish()
+    for copy in x_copies:
+        copy.wait()
+    mine.wait()
+
+
+def scatter_grads(g_sq, g_in, g_out, g_x, z_count):
+    n_sq = g_sq.shape[0]
+    order = [("square", n) for n in range(4, n_sq)]
+    order += [("rows", n) for n in range(4)] + [("cols", n) for n in range(4)]
+    order += [("square", n) for n in (3, 0, 1, 2)]
+    n = len(order)
+    vmem = pl.BlockSpec(memory_space=pltpu.VMEM)
+    hbm = pl.BlockSpec(memory_space=pltpu.HBM)
+    out_shape = [
+        jax.ShapeDtypeStruct((n_sq, ROWS // 2, 2 * HALF), f32),
+        jax.ShapeDtypeStruct((ROWS // 2, 8 * HALF), f32),
+        jax.ShapeDtypeStruct((2 * ROWS, 2 * HALF), f32),
+        jax.ShapeDtypeStruct(g_x.shape, bf16),
+    ]
+    return pl.pallas_call(
+        functools.partial(scatter_kernel, order, z_count),
+        out_shape=out_shape,
+        in_specs=[hbm] * 4,
+        out_specs=[vmem] * 3 + [hbm],
+        scratch_shapes=[
+            pltpu.VMEM((n, z_count, 4, ROWS, HALF), bf16),
+            pltpu.VMEM((4, z_count, 4, ROWS, HALF), bf16),
+            pltpu.VMEM((n, 2, z_count, ROWS, HALF), bf16),
+            pltpu.VMEM((n, z_count, ROWS, HALF), bf16),
+            pltpu.VMEM((n, z_count - 1, ROWS, HALF), bf16),
+            pltpu.VMEM((n, ROWS, HALF), f32),
+            pltpu.VMEM((n, ROWS, HALF), f32),
+            pltpu.SemaphoreType.DMA((n, 8)),
+            pltpu.SemaphoreType.DMA((n, 8)),
+            pltpu.SemaphoreType.DMA((n,)),
+            pltpu.SemaphoreType.DMA((3,)),
+            pltpu.SemaphoreType.DMA((3,)),
+            pltpu.SemaphoreType.DMA((1,)),
+        ],
+        compiler_params=pltpu.CompilerParams(
+            collective_id=1, has_side_effects=True, vmem_limit_bytes=60 * MIB
+        ),
+        name="scatter_grads",
+    )(g_sq, g_in, g_out, g_x)
+
+
+def total_kernel(z_count, in_ref, out_ref, acc, got, send, recv):
+    z, s, c = place()[:3]
+    greet(z, s, c, z_count)
+    started = []
+    slot = 0
+
+    def exchange(peers):
+        nonlocal slot
+        base = slot
+        for peer in peers:
+            copy = remote(acc, got.at[slot], send.at[slot], recv.at[slot], peer)
+            copy.start()
+            started.append(copy)
+            slot += 1
+        for copy in started[base:]:
+            copy.wait()
+        total = acc[...]
+        for k in range(base, slot):
+            total = total + got[k]
+        acc[...] = total
+
+    acc[...] = in_ref[...]
+    exchange([(z, s, 1 - c)])
+    exchange([(z, (s + d) % 4, c) for d in range(1, 4)])
+    exchange([((z + d) % z_count, s, c) for d in range(1, z_count)])
+    out_ref[...] = acc[...]
+
+
+def total_all(x, z_count):
+    vmem = pl.BlockSpec(memory_space=pltpu.VMEM)
+    slots = z_count + 3
+    return pl.pallas_call(
+        functools.partial(total_kernel, z_count),
+        out_shape=jax.ShapeDtypeStruct(x.shape, f32),
+        in_specs=[vmem],
+        out_specs=vmem,
+        scratch_shapes=[
+            pltpu.VMEM(x.shape, f32),
+            pltpu.VMEM((slots,) + x.shape, f32),
+            pltpu.SemaphoreType.DMA((slots,)),
+            pltpu.SemaphoreType.DMA((slots,)),
+        ],
+        compiler_params=pltpu.CompilerParams(collective_id=2, has_side_effects=True),
+        name="total_all",
+    )(x)
+
+
 def on_device(
     inputs,
     dec_in,
@@ -233,26 +754,45 @@
     rel_bias_m,
     rel_bias_v,
 ):
-    def gather_rows(x):
-        return lax.all_gather(x.astype(bf16), AXES, axis=x.ndim - 2, tiled=True)
-
-    sq_a = gather_rows(square[:4])
-    w_in_e = gather_rows(ffn_in[0])
-    w_out_e = gather_rows(ffn_out[0])
-    sq_b = gather_rows(jnp.stack([square[i] for i in (7, 8, 4, 5, 6, 9)]))
-    w_in_d = gather_rows(ffn_in[1])
-    w_out_d = gather_rows(ffn_out[1])
-    gain_f = lax.all_gather(gains.astype(bf16), AXES, axis=1, tiled=True).astype(f32)
-    w = {0: sq_a[0], 1: sq_a[1], 2: sq_a[2], 3: sq_a[3]}
-    for n, i in enumerate((7, 8, 4, 5, 6, 9)):
-        w[i] = sq_b[n]
+    z_count = lax.axis_size("dp")
+    width = inputs.shape[2]
+    direct = lax.axis_size("seq") == 4 and width == 2 * HALF and width == 4 * z_count * ROWS
+    w = {}
+    if direct:
+        gains_t = jnp.pad(gains.T, ((0, 0), (0, 128 - gains.shape[0])))
+        sq_g, in_g, out_g, gain_g, x_b = gather_weights(
+            square, ffn_in, ffn_out, gains_t, inputs, z_count
+        )
+        sq_g = sq_g.reshape(-1, width, width)
+        in_g = in_g.reshape(2, width, -1)
+        out_g = out_g.reshape(2, -1, width)
+        w_in_e, w_in_d = in_g[0], in_g[1]
+        w_out_e, w_out_d = out_g[0], out_g[1]
+        gain_f = gain_g.reshape(width, 128)[:, : gains.shape[0]].T.astype(f32)
+        x_b = x_b.reshape(-1, width)
+        for i in range(square.shape[0]):
+            w[i] = sq_g[i]
+    else:
+
+        def gather_rows(x):
+            return lax.all_gather(x.astype(bf16), AXES, axis=x.ndim - 2, tiled=True)
+
+        sq_a = gather_rows(square[:4])
+        w_in_e = gather_rows(ffn_in[0])
+        w_out_e = gather_rows(ffn_out[0])
+        sq_b = gather_rows(square[4:])
+        w_in_d = gather_rows(ffn_in[1])
+        w_out_d = gather_rows(ffn_out[1])
+        gain_f = lax.all_gather(gains.astype(bf16), AXES, axis=1, tiled=True).astype(f32)
+        for i in range(square.shape[0]):
+            w[i] = sq_a[i] if i < 4 else sq_b[i - 4]
+        x_b = lax.all_to_all(inputs, "seq", split_axis=0, concat_axis=1, tiled=True)[0]
 
     seq_pos = lax.axis_index("seq")
-    local_len, width = inputs.shape[1:]
+    local_len = inputs.shape[1]
     span = local_len * lax.axis_size("seq")
     bucket_count = rel_bias.shape[0]
     scale = 1.0 / math.sqrt(HD)
-    x_b = lax.all_to_all(inputs, "seq", split_axis=0, concat_axis=1, tiled=True)[0]
     x_f = x_b.astype(f32)
     length = lax.dynamic_slice_in_dim(lengths, seq_pos, 1, 0)
     key_valid = jnp.arange(span)[None, :] < length[:, None]
@@ -319,7 +859,9 @@
 
     lefts = (self_norm, self_values, cross_norm, cross_att, ffn_norm, inner_dec)
     rights = (g_self_values, g_one_b, g_cross_q, g_two_b, g_pre_dec, g_top_b)
-    packed = lax.all_gather(jnp.concatenate(lefts + rights, axis=1), AXES, axis=0, tiled=True)
+    own_row = jnp.concatenate(lefts + rights, axis=1)
+    own_row = jnp.pad(own_row, ((0, 0), (0, 20 * 1024 - own_row.shape[1])))
+    packed = lax.all_gather(own_row, AXES, axis=0, tiled=True)
     me = (
         lax.axis_index("dp") * lax.axis_size("seq") + seq_pos
     ) * lax.axis_size("head") + lax.axis_index("head")
@@ -355,19 +897,31 @@
     g_normed = mm_t(gq, w[0]) + mm_t(gk, w[1]) + mm_t(gv, w[2])
     g_input_norm, g_gain_zero = rms_pull(x_f, gain_f[0], g_normed)
     g_x = (g_hidden + g_input_norm).astype(bf16)
-    input_grad = lax.all_to_all(g_x[None], "seq", split_axis=1, concat_axis=0, tiled=True).astype(
-        f32
-    )
-
-    def scatter_rows(x):
-        return lax.psum_scatter(
-            x.astype(bf16), AXES, scatter_dimension=x.ndim - 2, tiled=True
+    if direct:
+        g_sq = jnp.stack([g.astype(bf16) for g in (g_w0, g_w1, g_w2, g_w3, g_w7, g_w8)])
+        s_sq, s_in, s_out, input_grad = scatter_grads(
+            g_sq.reshape(6, z_count, 4, ROWS, width),
+            g_in_e.astype(bf16).reshape(1, z_count, 4, ROWS, -1),
+            g_out_e.astype(bf16).reshape(1, z_count, 4, -1, width),
+            g_x.reshape(inputs.shape),
+            z_count,
+        )
+        s_0123, s_78 = s_sq[:4], s_sq[4:]
+        input_grad = input_grad.astype(f32)
+    else:
+        input_grad = lax.all_to_all(
+            g_x[None], "seq", split_axis=1, concat_axis=0, tiled=True
         ).astype(f32)
 
-    s_78 = scatter_rows(jnp.stack((g_w7, g_w8)))
-    s_out = scatter_rows(g_out_e)
-    s_in = scatter_rows(g_in_e)
-    s_0123 = scatter_rows(jnp.stack((g_w0, g_w1, g_w2, g_w3)))
+        def scatter_rows(x):
+            return lax.psum_scatter(
+                x.astype(bf16), AXES, scatter_dimension=x.ndim - 2, tiled=True
+            ).astype(f32)
+
+        s_78 = scatter_rows(jnp.stack((g_w7, g_w8)))
+        s_out = scatter_rows(g_out_e)
+        s_in = scatter_rows(g_in_e)
+        s_0123 = scatter_rows(jnp.stack((g_w0, g_w1, g_w2, g_w3)))
     summed_sq = jnp.stack(
         (
             s_0123[0],
@@ -387,15 +941,24 @@
     g_gains = jnp.stack(
         (g_gain_zero, g_gain_one, g_gain_two, g_gain_three, g_gain_four, g_gain_five)
     )
-    g_gains, g_bias = lax.psum((g_gains, g_bias_here), AXES)
     gain_share = gains.shape[1]
-    summed_gain = lax.dynamic_slice_in_dim(g_gains, me * gain_share, gain_share, 1)
     local_squares = (
         jnp.sum(summed_sq * summed_sq)
         + jnp.sum(summed_in * summed_in)
         + jnp.sum(summed_out * summed_out)
     )
-    shard_squares = lax.psum(local_squares, AXES)
+    if direct:
+        rest = jnp.concatenate((g_bias_here.reshape(-1), local_squares[None]))
+        rest = jnp.pad(rest, (0, 1024 - rest.shape[0])).reshape(8, 128)
+        wide = jnp.concatenate((jnp.pad(g_gains, ((0, 2), (0, 0))), rest), axis=1)
+        wide = total_all(wide, z_count)
+        g_gains = wide[:6, :width]
+        rest = wide[:, width:].reshape(-1)
+        g_bias = rest[: g_bias_here.size].reshape(g_bias_here.shape)
+        shard_squares = rest[g_bias_here.size]
+    else:
+        g_gains, g_bias, shard_squares = lax.psum((g_gains, g_bias_here, local_squares), AXES)
+    summed_gain = lax.dynamic_slice_in_dim(g_gains, me * gain_share, gain_share, 1)
     grad_norm = jnp.sqrt(shard_squares + jnp.sum(g_gains * g_gains) + jnp.sum(g_bias * g_bias))
     factor = clip_bound / jnp.maximum(grad_norm, clip_bound)
     return (

time: 945 us -> 519 us (0.55)
  waiting for transfers between devices: 557 us -> 0.04 us
  Pallas kernels: 52.2 us -> 334 us
  blocking collectives: 131 us -> 0 us
  matrix products: 107 us -> 73.1 us
  local copies, waits for them, and re-layouts: 30.6 us -> 53.2 us
  starting transfers between devices: 9.5 us -> 0.04 us
    all_gather x6 -> x1, waiting for transfers between devices: 287 us -> 0.02 us  [on_device(): packed = lax.all_gather(own_row, AXES, axis=0, tiled=True)]
    pallas_call x0 -> x3, Pallas kernels: none -> 282 us  [the longest x1 152 us: gather_weights(): pl.pallas_call(functools.partial(gather_kernel, order, z_count), out_shap...]
    reduce_scatter x2 -> x0, waiting for transfers between devices: 217 us -> none  [scatter_rows(): lax.psum_scatter(x.astype(bf16), AXES, scatter_dimension=x.ndim - 2, tile...]
    all_gather x2 -> x0, blocking collectives: 91 us -> none  [the longest x1 47.1 us: on_device(): lax.all_gather(jnp.concatenate(lefts + rights, axis=1), AXES, axis=0, til...]
    unnamed x12 -> x1, waiting for transfers between devices: 52.9 us -> 0.02 us
    psum x1 -> x0, blocking collectives: 40.5 us -> none  [on_device(): shard_squares = lax.psum(local_squares, AXES)]
    slice x6 -> x4, local copies, waits for them, and re-layouts: 2.15 us -> 25.9 us  [the longest x1 8.75 us: on_device(): w_in_e, w_in_d = (in_g[0], in_g[1])]
    dot_general x16, matrix products: 42.3 us -> 21.6 us  [matmul(): return jnp.dot(left, right, preferred_element_type=f32)]
  transfers between devices with their start and end apart: 12 -> 1, of which waited for: 9 -> 0; matrix products, arithmetic and copies ran while one was open for 13% -> 10% of each run, Pallas kernels for 6% -> 29%
where the time goes in v2:
time: 519 us; the launch traced here: 511 us
  Pallas kernels  334 us (64%)
  matrix products  73.1 us (14%)
  local copies, waits for them, and re-layouts  53.2 us (10%)
  between operations  25.2 us (5%)
  other arithmetic  24.9 us (5%)
    pallas_call x1, Pallas kernels, gather_weights(): pl.pallas_call(functools.partial(gather_kernel, order, z_count), out_shap...  152 us
    pallas_call x1, Pallas kernels, scatter_grads(): pl.pallas_call(functools.partial(scatter_kernel, order, z_count), out_sha...  118 us
    pallas_call x1, Pallas kernels, attend_bwd(): pl.pallas_call(attend_bwd_kernel, grid=(width // (2 * HD),), out_shape=(l...  33 us
    dot_general x16, matrix products, mm_t(): lax.dot_general(left, right, (((1,), (1,)), ((), ())), preferred_element_...  29.8 us
    dot_general x16, matrix products, matmul(): return jnp.dot(left, right, preferred_element_type=f32)  21.6 us
    unnamed x151, local copies, waits for them, and re-layouts  21.4 us
    dot_general x16, matrix products, mm_outer(): lax.dot_general(left, right, (((0,), (0,)), ((), ())), preferred_element_...  20.8 us
    pallas_call x1, Pallas kernels, attend_fwd(): pl.pallas_call(attend_fwd_kernel, grid=(width // (2 * HD),), out_shape=ja...  19.4 us
  transfers between devices with their start and end apart: 1, of which 0 were waited for; matrix products, arithmetic and copies ran while one was open for 10% of the time, Pallas kernels for 29%

profile of v2, /device:TPU:0, one launch (start us, length us, event | category | flops | bytes accessed | tf_op | source)
XLA Modules:
  0.0 510.8 jit_solution(15119820338500178097)
XLA Ops:
  7.2 1.3 fusion.101
  8.5 0.8 copy.91
  9.9 152.1 %gather_weights.1 = (bf16[10,4,4,48,768]{4,3,2,1,0:T(8,128)(2,1)}, bf16[2,4,4,48,3072]{4,3,2,1,0:T(8,128)(2,1)}, bf16[2,4,4,192,768]{4,3,2,1,0:T(8,128)(2,1)}, b...) custom-call(f32[10,24,768]{2,1,0:T(8,128)} %sq_ref.1, f32[2,24,3072]{2,1,0:T(8,128)} %in_ref.1, f32[2,96,768]{2,1,0:T(8,128)} %out_ref.1, ...), custom_call_target="tpu_custom_call" | custom-call | tf_op jit(solution)/shard_map/gather_weights/pallas_call | solution.py:448
  162.1 8.3 %fusion.124 = (bf16[1,4,4,48,768]{4,3,2,1,0:T(8,128)(2,1)}, bf16[1,4,4,48,768]{4,3,2,1,0:T(8,128)(2,1)}, bf16[1,4,4,48,768]{4,3,2,1,0:T(8,128)(2,1)}, bf16[1,4,4...) fusion(bf16[10,4,4,48,768]{4,3,2,1,0:T(8,128)(2,1)} %get-tuple-, ...), kind=kLoop, calls=%fused_computation.271 | loop fusion | bytes 23592960 | tf_op jit(solution)/shard_map/slice | solution.py:774
  173.5 0.8 convolution_convert_fusion.14.q_ref
  174.7 0.8 convolution_convert_fusion.13.k_ref
  176.0 0.8 convolution_convert_fusion.12.v_ref
  176.8 8.3 %fusion.125 = (bf16[1,4,4,192,768]{4,3,2,1,0:T(8,128)(2,1)}, bf16[1,4,4,192,768]{4,3,2,1,0:T(8,128)(2,1)}) fusion(bf16[2,4,4,192,768]{4,3,2,1,0:T(8,128)(2,1)} %get-tuple-element.35), kind=kLoop, calls=%fused_computation.272 | loop fusion | bytes 18874368 | tf_op jit(solution)/shard_map/slice | solution.py:770
  185.1 8.8 %fusion.126 = (bf16[1,4,4,48,3072]{4,3,2,1,0:T(8,128)(2,1)}, bf16[1,4,4,48,3072]{4,3,2,1,0:T(8,128)(2,1)}) fusion(bf16[2,4,4,48,3072]{4,3,2,1,0:T(8,128)(2,1)} %get-tuple-element.34), kind=kLoop, calls=%fused_computation.273 | loop fusion | bytes 18874368 | tf_op jit(solution)/shard_map/slice | solution.py:769
  194.4 19.4 %attend_fwd.1 = bf16[512,768]{1,0:T(8,128)(2,1)S(1)} custom-call(s32[1]{0:T(128)} %dynamic_slice.24.len_ref, f32[12,1,1024]{2,1,0:T(1,128)S(1)} %broadcast_in_dim.31.table_ref, bf16[512,768]{1,0:T(8,128)(2,1)S(1)} %convolution_convert_fusion.14.q_ref, bf16[512,768]{1,0:T(8,128)(2,1)S(1)} %convolution_convert_fusion.13.k_ref, ...), custom_call_target="tpu_custom_call" | custom-call | tf_op jit(solution)/shard_map/attend_fwd/pallas_call | solution.py:178
  213.8 2.5 multiply_reduce_fusion.5
  216.4 2.7 fusion.116
  219.1 3.8 multiply_reduce_fusion.4
  223.2 1.9 copy-done.19
  225.1 1.7 convolution_convert_fusion.10
  226.7 1.6 convolution_convert_fusion.11
  230.0 0.8 iota_compare_fusion.5
  230.8 1.6 convolution_reduce_fusion.5
  232.4 1.6 fusion.128
  236.1 3.2 fusion.97
  239.4 3.7 fusion.95
  243.1 4.3 fusion.117
  250.4 1.1 fusion.118
  252.1 0.8 convolution_reduce_fusion.2
  255.1 0.8 fusion.129
  256.6 1.1 multiply_reduce_fusion
  258.6 8.5 %fusion.6 = bf16[512,3072]{1,0:T(8,128)(2,1)S(1)} fusion(f32[512,3072]{1,0:T(8,128)S(1)} %bitcast.232, bf16[3072,768]{1,0:T(8,128)(2,1)} %bitcast.238, f32[512,768]{1,0:T(8,128)S(1)} %add_add_fusion.2), kind=kOutput, calls=%fused_computation.8 | convolution fusion | flops 2447769600 | bytes 15728640 | tf_op jit(solution)/shard_map/dot_general | solution.py:48
  267.2 2.9 multiply_reduce_fusion.1
  270.5 0.9 copy-done.30
  271.3 0.8 convolution_convert_fusion.8.do_ref
  272.2 33.0 %attend_bwd.1 = (bf16[512,768]{1,0:T(8,128)(2,1)S(1)}, bf16[512,768]{1,0:T(8,128)(2,1)S(1)}, bf16[512,768]{1,0:T(8,128)(2,1)S(1)}, f32[12,1,1024]{2,1,0:T(1,128)S(1)}) custom-call(s32[1]{0:T(128)} %dynamic_slice.24.len_ref, f32[12,1,1024]{2,1,0:T(1,128)S(1)} %broadcast_in_dim.31.table_ref, bf16[512,768]{1,0:T(8,128)(2,1)S(1)} %convolution_convert_fusion.14.q_ref, ...), custom_call_target="tpu_custom_call" | custom-call | tf_op jit(solution)/shard_map/attend_bwd/pallas_call | solution.py:196
  305.2 0.8 fusion.130
  306.5 0.8 fusion.131
  308.0 1.2 fusion.13
  309.3 1.5 fusion.9
  310.8 0.8 convolution_convert_fusion.7
  311.6 0.8 convolution_convert_fusion.6
  312.4 0.8 convolution_convert_fusion.5
  313.3 0.8 convolution_convert_fusion.4
  314.4 1.9 convolution_convert_fusion.3
  316.3 0.8 convolution_convert_fusion.2
  317.1 1.1 copy-done.55
  318.1 4.7 convolution_convert_fusion.1
  322.8 1.1 constant_dynamic-update-slice_fusion.5
  323.9 1.1 constant_dynamic-update-slice_fusion.4
  325.0 1.1 constant_dynamic-update-slice_fusion.3
  326.1 1.1 constant_dynamic-update-slice_fusion.2
  327.8 2.4 constant_dynamic-update-slice_fusion.1
  330.2 1.1 constant_dynamic-update-slice_fusion.sq_ref
  332.0 8.3 %convolution_convert_fusion = bf16[3072,768]{1,0:T(8,128)(2,1)} fusion(f32[512,768]{1,0:T(8,128)S(1)} %copy-done.14, f32[512,3072]{1,0:T(8,128)} %copy-done.12), kind=kOutput, calls=%fused_computation.10 | convolution fusion | flops 2432827392 | bytes 12582912 | tf_op jit(solution)/shard_map/dot_general | solution.py:52
  340.4 117.5 %scatter_grads.1 = (f32[6,24,768]{2,1,0:T(8,128)}, f32[24,3072]{1,0:T(8,128)}, f32[96,768]{1,0:T(8,128)}, bf16[4,128,768]{2,1,0:T(8,128)(2,1)}) custom-call(bf16[6,4,4,48,768]{4,3,2,1,0:T(8,128)(2,1)} %constant_dynamic-update-slice_fusion.sq_ref, bf16[1,4,4,48,3072]{4,3,2,1,0:T(8,128)(2,1)} %bitcast.242, bf16[1,4,4,192,768]{4,3,2,1,0:T(8,128)(2,1)} %bitcast.243, ...), custom_call_target="tpu_custom_call" | custom-call | tf_op jit(solution)/shard_map/scatter_grads/pallas_call | solution.py:661
  458.0 2.5 convert_element_type.289
  461.9 1.0 constant_dynamic-slice_fusion.1
  463.1 3.2 copy.120
  467.0 0.8 multiply_reduce_fusion.6
  468.0 0.9 constant_dynamic-slice_fusion
  469.1 1.7 multiply_reduce_fusion.8
  472.1 1.7 multiply_reduce_fusion.7
  475.1 12.2 %total_all.1 = f32[8,896]{1,0:T(8,128)} custom-call(f32[8,896]{1,0:T(8,128)} %select_maximum_fusion.in_ref), custom_call_target="tpu_custom_call" | custom-call | tf_op jit(solution)/shard_map/total_all/pallas_call | solution.py:719
  488.0 1.3 fusion.127
  489.4 1.3 multiply_reduce_fusion.15
  494.1 3.2 multiply_subtract_fusion
  497.4 1.5 multiply_subtract_fusion.2
  499.5 1.5 multiply_subtract_fusion.1
  (228 shorter events, 22.4 us)
Async XLA Ops:
  7.2 454.7 %all-gather.3.cloned.1.call-start = ((), (), s32[]{:S(2)}) async-start(), calls=%async_computation | async-start | bytes 2703360 | tf_op jit(solution)/shard_map/all_gather | solution.py:864
  162.0 8.4 %copy-start.43 = (bf16[4,4,48,128]{3,2,1,0:T(8,128)(2,1)S(1)}, bf16[4,4,48,128]{3,2,1,0:T(8,128)(2,1)}, u32[]{:S(2)}) copy-start(bf16[4,4,48,128]{3,2,1,0:T(8,128)(2,1)} %get-tuple-element.31) | copy-start | bytes 589828
  162.1 10.0 %copy-start.44 = (bf16[1,1,768]{2,1,0:T(2,128)(2,1)S(1)}, bf16[1,1,768]{2,1,0:T(2,128)(2,1)}, u32[]{:S(2)}) copy-start(bf16[1,1,768]{2,1,0:T(2,128)(2,1)} %param.21) | copy-start | bytes 4612
  162.1 10.3 %copy-start.50 = (s32[1023]{0:T(1024)S(1)}, s32[1023]{0:T(1024)}, u32[]{:S(2)}) copy-start(s32[1023]{0:T(1024)} %param.24) | copy-start | bytes 12280
  162.1 10.3 %copy-start.47 = (f32[32,12]{0,1:T(8,128)S(1)}, f32[32,12]{0,1:T(8,128)}, u32[]{:S(2)}) copy-start(f32[32,12]{0,1:T(8,128)} %param.37) | copy-start | bytes 4612
  170.4 3.0 copy-start.5
  170.4 3.0 copy-start.28
  170.4 2.5 copy-start.3
  173.4 1.3 copy-start.26
  174.7 1.3 copy-start.17
  185.1 8.8 %copy-start.53 = (s32[4]{0:T(128)S(1)}, s32[4]{0:T(128)}, u32[]{:S(2)}) copy-start(s32[4]{0:T(128)} %param.23) | copy-start | bytes 52
  194.4 22.0 %copy-start = (bf16[1,4,4,48,3072]{4,3,2,1,0:T(8,128)(2,1)S(1)}, bf16[1,4,4,48,3072]{4,3,2,1,0:T(8,128)(2,1)}, u32[]{:S(2)}) copy-start(bf16[1,4,4,48,3072]{4,3,2,1,0:T(8,128)(2,1)} %get-tuple-element.145) | copy-start | bytes 14155780
  213.8 5.2 %slice-start.6 = ((s8[4718592]{0:T(1024)(128)(4,1)}), s8[4194304]{0:T(1024)(128)(4,1)S(1)}, s32[]{:S(2)}) async-start(s8[4718592]{0:T(1024)(128)(4,1)} %bitcast.239), calls=%async_computation.7 | async-start | bytes 8388608
  216.3 2.7 copy-start.15
  216.4 2.7 slice-start.7
  219.0 3.9 copy-start.12
  222.9 3.8 copy-start.1
  222.9 2.1 copy-start.19
  223.2 3.6 copy-start.36
  225.1 1.7 copy-start.31
  226.7 1.7 copy-start.7
  229.9 4.2 copy-start.21
  229.9 4.5 copy-start.10
  236.1 3.2 copy-start.45
  236.1 11.3 %slice-start = ((s8[4718592]{0:T(1024)(128)(4,1)}), s8[4194304]{0:T(1024)(128)(4,1)S(1)}, s32[]{:S(2)}) async-start(s8[4718592]{0:T(1024)(128)(4,1)} %bitcast.214), calls=%async_computation.1 | async-start | bytes 8388608
  239.4 8.1 %slice-start.1 = ((s8[4718592]{0:T(1024)(128)(4,1)}), s8[524288]{0:T(1024)(128)(4,1)S(1)}, s32[]{:S(2)}) async-start(s8[4718592]{0:T(1024)(128)(4,1)} %bitcast.214), calls=%async_computation.2 | async-start | bytes 1048576
  247.5 1.6 copy-start.11
  247.5 2.1 copy-start.22
  248.2 1.8 copy-start.35
  248.2 2.1 copy-start.9
  249.5 2.6 copy-start.8
  253.8 1.3 copy-start.32
  254.3 1.6 copy-start.20
  255.1 1.5 copy-start.2
  255.1 3.0 slice-start.4
  256.6 2.0 slice-start.5
  257.7 9.4 %slice-start.2 = ((s8[4718592]{0:T(1024)(128)(4,1)}), s8[4194304]{0:T(1024)(128)(4,1)S(1)}, s32[]{:S(2)}) async-start(s8[4718592]{0:T(1024)(128)(4,1)} %bitcast.220), calls=%async_computation.3 | async-start | bytes 8388608
  258.6 11.5 %copy-start.13 = (f32[512,768]{1,0:T(8,128)}, f32[512,768]{1,0:T(8,128)S(1)}, u32[]{:S(2)}) copy-start(f32[512,768]{1,0:T(8,128)S(1)} %add_add_fusion.2) | copy-start | bytes 4718596
  258.6 8.5 %slice-start.3 = ((s8[4718592]{0:T(1024)(128)(4,1)}), s8[524288]{0:T(1024)(128)(4,1)S(1)}, s32[]{:S(2)}) async-start(s8[4718592]{0:T(1024)(128)(4,1)} %bitcast.220), calls=%async_computation.4 | async-start | bytes 1048576
  258.6 8.5 %copy-start.16 = (f32[512,768]{1,0:T(8,128)S(1)}, f32[512,768]{1,0:T(8,128)}, u32[]{:S(2)}) copy-start(f32[512,768]{1,0:T(8,128)} %copy-done.15) | copy-start | bytes 4718596
  267.1 2.9 copy-start.54
  270.1 1.3 copy-start.30
  272.2 33.0 %copy-start.29 = (bf16[1,4,4,48,768]{4,3,2,1,0:T(8,128)(2,1)S(1)}, bf16[1,4,4,48,768]{4,3,2,1,0:T(8,128)(2,1)}, u32[]{:S(2)}) copy-start(bf16[1,4,4,48,768]{4,3,2,1,0:T(8,128)(2,1)} %copy-done.28) | copy-start | bytes 3538948
  305.2 1.3 copy-start.27
  306.5 1.1 copy-start.4
  306.5 1.5 copy-start.18
  316.3 1.9 copy-start.55
  330.2 1.8 copy-start.14
  457.9 2.6 copy-start.6
  457.9 3.9 copy-start.42
  467.0 27.1 %copy-start.23 = (f32[10,24,768]{2,1,0:T(8,128)S(1)}, f32[10,24,768]{2,1,0:T(8,128)}, u32[]{:S(2)}) copy-start(f32[10,24,768]{2,1,0:T(8,128)} %sq_ref.1) | copy-start | bytes 2211844
  494.1 3.2 copy-start.24
  494.1 3.2 copy-start.34
  494.1 3.2 copy-start.38
  494.1 3.2 copy-start.39
  497.3 1.6 copy-start.25
  497.4 1.6 copy-start.33
  497.4 1.7 copy-start.40
  497.4 2.1 copy-start.41
  499.5 1.6 copy-start.48
  499.5 1.6 copy-start.49
  499.5 2.2 copy-start.46
  499.5 2.2 copy-start.51
  499.5 2.2 copy-start.52
  (1 other events, 1.1 us)
Sparse Core Ops, SparseCore 0:
  253.9 58.7 all-gather.2

commit v3 on v2

--- a/solution.py
+++ b/solution.py
@@ -335,15 +335,62 @@
             copy.wait_send()
 
 
-def gather_kernel(
-    units, z_count, sq_ref, in_ref, out_ref, gain_ref, x_ref,
-    sq_o, in_o, out_o, gain_o, x_o,
-    sq_w, in_w, out_w, gain_w, sq_r, in_r, out_r, gain_r,
-    send, recv, first_send, first_recv, x_send, x_recv, local,
-):
+def row_blocks(count, work):
+    def body(i, carry):
+        work(i, pl.ds(pl.multiple_of(i * BAND, BAND), BAND))
+        return carry
+
+    lax.fori_loop(0, count, body, 0)
+
+
+def col_tiles(width, tile, work):
+    def body(i, carry):
+        work(pl.ds(pl.multiple_of(i * tile, tile), tile))
+        return carry
+
+    lax.fori_loop(0, width // tile, body, 0)
+
+
+def wide(value):
+    return value.reshape(value.shape[0] * value.shape[1] * value.shape[2], value.shape[3])
+
+
+def attend_pair_fwd(pair, length, table_ref, q_ref, k_ref, v_ref, o_ref):
+    span = k_ref.shape[0]
+    at = pl.ds(pl.multiple_of(pair * 2 * HD, 2 * HD), 2 * HD)
+    valid = lax.broadcasted_iota(jnp.int32, (1, span), 1) < length
+    lane = lax.broadcasted_iota(jnp.int32, (1, 2 * HD), 1)
+    k_all = k_ref[:, at]
+    v_all = v_ref[:, at]
+    bands = [bias_band(table_ref[2 * pair + t], span) for t in range(2)]
+    for block in range(span // BAND):
+        rows = slice(block * BAND, (block + 1) * BAND)
+        q_rows = q_ref[rows, at]
+        parts = []
+        for t in range(2):
+            own = (lane // HD) == t
+            probs = softmax_rows(
+                jnp.where(own, q_rows, jnp.zeros_like(q_rows)), k_all, bands[t], block, span, valid
+            )
+            parts.append(matmul(probs.astype(bf16), v_all))
+        o_ref[rows, at] = jnp.where(lane < HD, parts[0], parts[1]).astype(bf16)
+
+
+def forward_kernel(units, z_count, *refs):
+    (
+        len_ref, table_ref, sq_ref, in_ref, out_ref, gain_ref, x_ref,
+        in_o, out_o, in_d, out_d, gain_o, x_o, q_o, k_o, v_o, att_o, hid_o, pre_o,
+        hid2_o, enc_o, ck_o, cv_o,
+        sq_o0, sq_o1, sq_o2, sq_o3, sq_o4, sq_o5, sq_o6, sq_o7, sq_o8, sq_o9,
+        sq_w, in_w, out_w, gain_w, sq_r, in_r, out_r, gain_r,
+        x_s, n_s, q_s, k_s, v_s, att_s, hid_s, pre_s, inner_s, hid2_s, enc_s, ck_s, cv_s, gains,
+        send, recv, first_send, first_recv, x_send, x_recv, local,
+    ) = refs
     z, s, c = place()[:3]
     sibling = (z, s, 1 - c)
+    sq_o = (sq_o0, sq_o1, sq_o2, sq_o3, sq_o4, sq_o5, sq_o6, sq_o7, sq_o8, sq_o9)
     n_sq, n_ff = sq_ref.shape[0], in_ref.shape[0]
+    blocks = x_s.shape[0] * x_s.shape[1] // BAND
     greet(z, s, c, z_count)
 
     first = []
@@ -355,41 +402,25 @@
 
     to_sibling(gain_ref, gain_r)
     to_sibling(sq_ref.at[:, :, cols(1 - c)], sq_r)
+    x_copies = []
+    for d in range(1, 4):
+        peer = (s + d) % 4
+        copy = remote(
+            x_ref.at[peer], x_s.at[s], x_send.at[d - 1], x_recv.at[d - 1], (z, peer, c)
+        )
+        copy.start()
+        x_copies.append(copy)
+    mine = pltpu.make_async_copy(x_ref.at[s], x_s.at[s], local.at[0])
+    mine.start()
     for n in range(n_ff):
         for j in range(4):
             to_sibling(in_ref.at[n, :, cols(1 - c, 2 * HALF * j)], in_r.at[n, j])
         to_sibling(out_ref.at[n, :, cols(1 - c)], out_r.at[n])
-    x_copies = []
-    for d in range(1, 4):
-        peer = (s + d) % 4
-        copy = remote(
-            x_ref.at[peer], x_o.at[s], x_send.at[d - 1], x_recv.at[d - 1], (z, peer, c)
-        )
-        copy.start()
-        x_copies.append(copy)
-    mine = pltpu.make_async_copy(x_ref.at[s], x_o.at[s], local.at[0])
-    mine.start()
 
     def joined(own, other):
         top = jnp.where(c == 0, own, other)
         bottom = jnp.where(c == 0, other, own)
         return jnp.concatenate([top, bottom], axis=0).astype(bf16)
-
-    first[0].wait_recv()
-    gain_w[z, s] = joined(gain_ref[...], gain_r[...])
-    first[1].wait_recv()
-    for n in range(n_sq):
-        sq_w[n, z, s, :, cols(c)] = joined(sq_ref[n, :, cols(c)], sq_r[n])
-    k = 2
-    for n in range(n_ff):
-        for j in range(4):
-            first[k].wait_recv()
-            k += 1
-            at = cols(c, 2 * HALF * j)
-            in_w[n, z, s, :, at] = joined(in_ref[n, :, at], in_r[n, j])
-        first[k].wait_recv()
-        k += 1
-        out_w[n, z, s, :, cols(c)] = joined(out_ref[n, :, cols(c)], out_r[n])
 
     gather = Gather(
         units,
@@ -398,81 +429,187 @@
         recv,
         z_count,
     )
-    outs = {"square": sq_o, "cols": in_o, "rows": out_o, "gain": gain_o}
+    first[0].wait_recv()
+    gain_w[z, s] = joined(gain_ref[...], gain_r[...])
+    first[1].wait_recv()
+    for n in range(n_sq):
+        sq_w[n, z, s, :, cols(c)] = joined(sq_ref[n, :, cols(c)], sq_r[n])
     drains = []
+
+    def drain(src, dst):
+        copy = pltpu.make_async_copy(src, dst, local.at[1 + len(drains)])
+        copy.start()
+        drains.append(copy)
 
     def done(u):
         kind, n = units[u]
         if kind == "square":
-            src, dst = sq_w.at[n], sq_o.at[n]
-        elif kind == "gain":
-            src, dst = gain_w, gain_o
-        elif n % 4 != 3:
-            return
-        elif kind == "cols":
-            src, dst = in_w.at[n // 4], in_o.at[n // 4]
-        else:
-            src, dst = out_w.at[n // 4], out_o.at[n // 4]
-        copy = pltpu.make_async_copy(src, dst, local.at[1 + len(drains)])
-        copy.start()
-        drains.append(copy)
-
-    del outs
+            drain(sq_w.at[n], sq_o[n])
+        elif kind == "cols" and n % 4 == 3:
+            drain(in_w.at[n // 4], (in_o, in_d)[n // 4])
+        elif kind == "rows" and n % 4 == 3:
+            drain(out_w.at[n // 4], (out_o, out_d)[n // 4])
+
+    def normed(src, gain_row, dst):
+        def work(i, at):
+            dst[at, :] = rms_gain(src(i, at), gains[gain_row : gain_row + 1, :]).astype(bf16)
+
+        row_blocks(blocks, work)
+
+    def x_rows(i, at):
+        return x_s[i].astype(f32)
+
+    def start_piece():
+        for copy in x_copies:
+            copy.wait_recv()
+        mine.wait()
+        drain(x_s, x_o)
+        gains[...] = wide(gain_w[...]).astype(f32).T[:8]
+        drain(gains, gain_o)
+        normed(x_rows, 0, n_s)
+
+    def square_dot(left, n, tile=256):
+        def weight(at):
+            return wide(sq_w[n, :, :, :, at])
+
+        return lambda at: matmul(left[...], weight(at))
+
+    def project(n, left, dst, out):
+        dot = square_dot(left, n)
+
+        def work(at):
+            dst[:, at] = dot(at).astype(bf16)
+
+        col_tiles(2 * HALF, 256, work)
+        drain(dst, out)
+
+    def attention(pairs):
+        def body(pair, carry):
+            attend_pair_fwd(pair, len_ref[0], table_ref, q_s, k_s, v_s, att_s)
+            return carry
+
+        lax.fori_loop(pairs[0], pairs[1], body, 0)
+
+    def hidden_piece():
+        drain(att_s, att_o)
+        dot = square_dot(att_s, 3)
+
+        def work(at):
+            hid_s[:, at] = dot(at)
+
+        col_tiles(2 * HALF, 256, work)
+
+        def add(i, at):
+            total = hid_s[at, :] + x_rows(i, at)
+            hid_s[at, :] = total
+            n_s[at, :] = rms_gain(total, gains[1:2, :]).astype(bf16)
+
+        row_blocks(blocks, add)
+        drain(hid_s, hid_o)
+
+    def ffn_piece(j):
+        def work(i, carry):
+            at = pl.ds(pl.multiple_of(j * 2 * HALF + i * 256, 256), 256)
+            pre = matmul(n_s[...], wide(in_w[0, :, :, :, at]))
+            pre_s[:, at] = pre
+            inner_s[:, at] = gelu_tanh(pre).astype(bf16)
+            return carry
+
+        lax.fori_loop(0, 3, work, 0)
+
+    def hidden_two_piece():
+        drain(pre_s, pre_o)
+
+        def work(at):
+            hid2_s[:, at] = hid_s[:, at] + matmul(inner_s[...], wide(out_w[0, :, :, :, at]))
+
+        col_tiles(2 * HALF, 256, work)
+        normed(lambda i, at: hid2_s[at, :], 2, enc_s)
+        drain(hid2_s, hid2_o)
+        drain(enc_s, enc_o)
+
     skew = 2
+    pieces = {
+        6: [start_piece],
+        9: [lambda: project(0, n_s, q_s, q_o)],
+        10: [lambda: project(1, n_s, k_s, k_o)],
+        11: [lambda: project(2, n_s, v_s, v_o), lambda: attention((0, 2))],
+        12: [lambda: attention((2, 4))],
+        13: [lambda: attention((4, 6))],
+        14: [hidden_piece, lambda: ffn_piece(0)],
+        15: [lambda: ffn_piece(1), lambda: ffn_piece(2)],
+        16: [lambda: ffn_piece(3)],
+        20: [hidden_two_piece],
+        21: [lambda: project(7, enc_s, ck_s, ck_o)],
+        22: [lambda: project(8, enc_s, cv_s, cv_o)],
+    }
+    k = 2
     for t in range(len(units) + 4 * skew):
         gather.tick(t, skew, done)
+        if t == 1:
+            for n in range(n_ff):
+                for j in range(4):
+                    first[k].wait_recv()
+                    k += 1
+                    at = cols(c, 2 * HALF * j)
+                    in_w[n, z, s, :, at] = joined(in_ref[n, :, at], in_r[n, j])
+                first[k].wait_recv()
+                k += 1
+                out_w[n, z, s, :, cols(c)] = joined(out_ref[n, :, cols(c)], out_r[n])
+        for piece in pieces.get(t, ()):
+            piece()
     gather.finish()
     for copy in first:
         copy.wait_send()
     for copy in x_copies:
-        copy.wait()
-    mine.wait()
+        copy.wait_send()
     for copy in drains:
         copy.wait()
 
 
-def gather_weights(square, ffn_in, ffn_out, gains_t, x, z_count):
+def forward(length, table, square, ffn_in, ffn_out, gains_t, x, z_count):
     n_sq, n_ff = square.shape[0], ffn_in.shape[0]
     order = [("gain", 0)]
     order += [("square", n) for n in (0, 1, 2, 3)]
     order += [("cols", n) for n in range(4)] + [("rows", n) for n in range(4)]
     order += [("square", n) for n in (7, 8, 4, 5, 6, 9)]
     order += [("cols", n) for n in range(4, 8)] + [("rows", n) for n in range(4, 8)]
-    sq_s = (n_sq, z_count, 4, ROWS, 2 * HALF)
-    in_s = (n_ff, z_count, 4, ROWS, 8 * HALF)
-    out_s = (n_ff, z_count, 4, 4 * ROWS, 2 * HALF)
+    blocks, band, width = x.shape
+    span = blocks * band
+    hidden_units = 8 * HALF
+    sq_s = (n_sq, z_count, 4, ROWS, width)
+    in_s = (n_ff, z_count, 4, ROWS, hidden_units)
+    out_s = (n_ff, z_count, 4, 4 * ROWS, width)
     gain_s = (z_count, 4, ROWS, 128)
     firsts = 2 + 5 * n_ff
     vmem = pl.BlockSpec(memory_space=pltpu.VMEM)
     hbm = pl.BlockSpec(memory_space=pltpu.HBM)
+    token = ((span, width), bf16)
+    token_f = ((span, width), f32)
+    outs = [(in_s[1:], bf16), (out_s[1:], bf16), (in_s[1:], bf16), (out_s[1:], bf16)]
+    outs += [((8, width), f32), (x.shape, bf16), token, token, token, token, token_f]
+    outs += [((span, hidden_units), f32), token_f, token, token, token]
+    outs += [(sq_s[1:], bf16)] * n_sq
+    scratch = [(sq_s, bf16), (in_s, bf16), (out_s, bf16), (gain_s, bf16)]
+    scratch += [((n_sq, ROWS // 2, HALF), f32), ((n_ff, 4, ROWS // 2, HALF), f32)]
+    scratch += [((n_ff, 2 * ROWS, HALF), f32), ((ROWS // 2, 128), f32)]
+    scratch += [(x.shape, bf16), token, token, token, token, token, token_f]
+    scratch += [((span, hidden_units), f32), ((span, hidden_units), bf16), token_f]
+    scratch += [token, token, token, ((8, width), f32)]
+    dma = pltpu.SemaphoreType.DMA
     return pl.pallas_call(
-        functools.partial(gather_kernel, order, z_count),
-        out_shape=[jax.ShapeDtypeStruct(shape, bf16) for shape in (sq_s, in_s, out_s, gain_s)]
-        + [jax.ShapeDtypeStruct(x.shape, bf16)],
-        in_specs=[vmem] * 4 + [hbm],
-        out_specs=[hbm] * 5,
-        scratch_shapes=[
-            pltpu.VMEM(sq_s, bf16),
-            pltpu.VMEM(in_s, bf16),
-            pltpu.VMEM(out_s, bf16),
-            pltpu.VMEM(gain_s, bf16),
-            pltpu.VMEM((n_sq, ROWS // 2, HALF), f32),
-            pltpu.VMEM((n_ff, 4, ROWS // 2, HALF), f32),
-            pltpu.VMEM((n_ff, 2 * ROWS, HALF), f32),
-            pltpu.VMEM((ROWS // 2, 128), f32),
-            pltpu.SemaphoreType.DMA((len(order), 7)),
-            pltpu.SemaphoreType.DMA((len(order), 7)),
-            pltpu.SemaphoreType.DMA((firsts,)),
-            pltpu.SemaphoreType.DMA((firsts,)),
-            pltpu.SemaphoreType.DMA((3,)),
-            pltpu.SemaphoreType.DMA((3,)),
-            pltpu.SemaphoreType.DMA((20,)),
-        ],
+        functools.partial(forward_kernel, order, z_count),
+        out_shape=[jax.ShapeDtypeStruct(*o) for o in outs],
+        in_specs=[pl.BlockSpec(memory_space=pltpu.SMEM)] + [vmem] * 5 + [hbm],
+        out_specs=[hbm] * len(outs),
+        scratch_shapes=[pltpu.VMEM(*o) for o in scratch]
+        + [dma((len(order), 7)), dma((len(order), 7)), dma((firsts,)), dma((firsts,))]
+        + [dma((3,)), dma((3,)), dma((40,))],
         compiler_params=pltpu.CompilerParams(
-            collective_id=0, has_side_effects=True, vmem_limit_bytes=60 * MIB
+            collective_id=0, has_side_effects=True, vmem_limit_bytes=62 * MIB
         ),
-        name="gather_weights",
-    )(square, ffn_in, ffn_out, gains_t, x)
+        name="forward",
+    )(length, table, square, ffn_in, ffn_out, gains_t, x)
 
 
 class Scatter:
@@ -757,21 +894,39 @@
     z_count = lax.axis_size("dp")
     width = inputs.shape[2]
     direct = lax.axis_size("seq") == 4 and width == 2 * HALF and width == 4 * z_count * ROWS
+    direct = direct and inputs.shape[:2] == (4, BAND)
     w = {}
+    seq_pos = lax.axis_index("seq")
+    local_len = inputs.shape[1]
+    span = local_len * lax.axis_size("seq")
+    bucket_count = rel_bias.shape[0]
+    scale = 1.0 / math.sqrt(HD)
+    length = lax.dynamic_slice_in_dim(lengths, seq_pos, 1, 0)
+    key_valid = jnp.arange(span)[None, :] < length[:, None]
+    one_hot = (
+        jnp.pad(bucket_table, (0, 1), constant_values=-1)[:, None]
+        == jnp.arange(bucket_count)[None, :]
+    ).astype(f32)
+    table = jnp.einsum("ob,bh->ho", one_hot, rel_bias, precision=highest_precision)[:, None, :]
+
     if direct:
         gains_t = jnp.pad(gains.T, ((0, 0), (0, 128 - gains.shape[0])))
-        sq_g, in_g, out_g, gain_g, x_b = gather_weights(
-            square, ffn_in, ffn_out, gains_t, inputs, z_count
+        outs = forward(length, table, square, ffn_in, ffn_out, gains_t, inputs, z_count)
+        w_in_e, w_out_e, w_in_d, w_out_d = (
+            outs[0].reshape(width, -1),
+            outs[1].reshape(-1, width),
+            outs[2].reshape(width, -1),
+            outs[3].reshape(-1, width),
         )
-        sq_g = sq_g.reshape(-1, width, width)
-        in_g = in_g.reshape(2, width, -1)
-        out_g = out_g.reshape(2, -1, width)
-        w_in_e, w_in_d = in_g[0], in_g[1]
-        w_out_e, w_out_d = out_g[0], out_g[1]
-        gain_f = gain_g.reshape(width, 128)[:, : gains.shape[0]].T.astype(f32)
-        x_b = x_b.reshape(-1, width)
+        gain_f = outs[4][: gains.shape[0]]
+        x_b = outs[5].reshape(-1, width)
+        q, k, v, attended, hidden, pre_act, hidden_two, encoded, cross_k, cross_v = outs[6:16]
         for i in range(square.shape[0]):
-            w[i] = sq_g[i]
+            w[i] = outs[16 + i].reshape(width, width)
+        x_f = x_b.astype(f32)
+        normed = rms_gain(x_f, gain_f[0]).astype(bf16)
+        normed_two = rms_gain(hidden, gain_f[1]).astype(bf16)
+        inner_act = gelu_tanh(pre_act).astype(bf16)
     else:
 
         def gather_rows(x):
@@ -787,34 +942,20 @@
         for i in range(square.shape[0]):
             w[i] = sq_a[i] if i < 4 else sq_b[i - 4]
         x_b = lax.all_to_all(inputs, "seq", split_axis=0, concat_axis=1, tiled=True)[0]
-
-    seq_pos = lax.axis_index("seq")
-    local_len = inputs.shape[1]
-    span = local_len * lax.axis_size("seq")
-    bucket_count = rel_bias.shape[0]
-    scale = 1.0 / math.sqrt(HD)
-    x_f = x_b.astype(f32)
-    length = lax.dynamic_slice_in_dim(lengths, seq_pos, 1, 0)
-    key_valid = jnp.arange(span)[None, :] < length[:, None]
-    one_hot = (
-        jnp.pad(bucket_table, (0, 1), constant_values=-1)[:, None]
-        == jnp.arange(bucket_count)[None, :]
-    ).astype(f32)
-    table = jnp.einsum("ob,bh->ho", one_hot, rel_bias, precision=highest_precision)[:, None, :]
-
-    normed = rms_gain(x_f, gain_f[0]).astype(bf16)
-    q = matmul(normed, w[0]).astype(bf16)
-    k = matmul(normed, w[1]).astype(bf16)
-    v = matmul(normed, w[2]).astype(bf16)
-    attended = attend_fwd(length, table, q, k, v)
-    hidden = x_f + matmul(attended, w[3])
-    normed_two = rms_gain(hidden, gain_f[1]).astype(bf16)
-    pre_act = matmul(normed_two, w_in_e)
-    inner_act = gelu_tanh(pre_act).astype(bf16)
-    hidden_two = hidden + matmul(inner_act, w_out_e)
-    encoded = rms_gain(hidden_two, gain_f[2]).astype(bf16)
-    cross_k = matmul(encoded, w[7]).astype(bf16)
-    cross_v = matmul(encoded, w[8]).astype(bf16)
+        x_f = x_b.astype(f32)
+        normed = rms_gain(x_f, gain_f[0]).astype(bf16)
+        q = matmul(normed, w[0]).astype(bf16)
+        k = matmul(normed, w[1]).astype(bf16)
+        v = matmul(normed, w[2]).astype(bf16)
+        attended = attend_fwd(length, table, q, k, v)
+        hidden = x_f + matmul(attended, w[3])
+        normed_two = rms_gain(hidden, gain_f[1]).astype(bf16)
+        pre_act = matmul(normed_two, w_in_e)
+        inner_act = gelu_tanh(pre_act).astype(bf16)
+        hidden_two = hidden + matmul(inner_act, w_out_e)
+        encoded = rms_gain(hidden_two, gain_f[2]).astype(bf16)
+        cross_k = matmul(encoded, w[7]).astype(bf16)
+        cross_v = matmul(encoded, w[8]).astype(bf16)
 
     dec_row = dec_in.reshape(1, width).astype(f32)
     self_norm = rms_gain(dec_row, gain_f[3]).astype(bf16)

time: 519 us -> 468 us (0.902)
  local copies, waits for them, and re-layouts: 53.2 us -> 32.5 us
  matrix products: 73.1 us -> 57.7 us
  Pallas kernels: 334 us -> 319 us
    slice x4 -> x0, local copies, waits for them, and re-layouts: 25.4 us -> none  [the longest x1 8.75 us: on_device(): w_in_e, w_in_d = (in_g[0], in_g[1])]
    pallas_call x2 -> x1, Pallas kernels: 172 us -> 158 us  [forward(): pl.pallas_call(functools.partial(forward_kernel, order, z_count), out_sha...]
    dot_general x16 -> x8, matrix products: 21.6 us -> 8.29 us  [matmul(): return jnp.dot(left, right, preferred_element_type=f32)]
    dot_general x16, matrix products: 29.8 us -> 24.5 us  [mm_t(): lax.dot_general(left, right, (((1,), (1,)), ((), ())), preferred_element_...]
    unnamed x151 -> x144, local copies, waits for them, and re-layouts: 21.4 us -> 22.9 us
  transfers between devices with their start and end apart: 1 -> 1, of which waited for: 0 -> 0; matrix products, arithmetic and copies ran while one was open for 10% -> 11% of each run, Pallas kernels for 29% -> 32%
where the time goes in v3:
time: 468 us; the launch traced here: 459 us
  Pallas kernels  319 us (68%)
  matrix products  57.7 us (12%)
  local copies, waits for them, and re-layouts  32.5 us (7%)
  other arithmetic  24.9 us (5%)
  between operations  24.1 us (5%)
    pallas_call x1, Pallas kernels, forward(): pl.pallas_call(functools.partial(forward_kernel, order, z_count), out_sha...  158 us
    pallas_call x1, Pallas kernels, scatter_grads(): pl.pallas_call(functools.partial(scatter_kernel, order, z_count), out_sha...  116 us
    pallas_call x1, Pallas kernels, attend_bwd(): pl.pallas_call(attend_bwd_kernel, grid=(width // (2 * HD),), out_shape=(l...  33.1 us
    dot_general x16, matrix products, mm_t(): lax.dot_general(left, right, (((1,), (1,)), ((), ())), preferred_element_...  24.5 us
    dot_general x16, matrix products, mm_outer(): lax.dot_general(left, right, (((0,), (0,)), ((), ())), preferred_element_...  23.2 us
    unnamed x144, local copies, waits for them, and re-layouts  22.9 us
    pallas_call x1, Pallas kernels, total_all(): pl.pallas_call(functools.partial(total_kernel, z_count), out_shape=jax.Sh...  12.8 us
  transfers between devices with their start and end apart: 1, of which 0 were waited for; matrix products, arithmetic and copies ran while one was open for 11% of the time, Pallas kernels for 32%

profile of v3, /device:TPU:0, one launch (start us, length us, event | category | flops | bytes accessed | tf_op | source)
XLA Modules:
  0.0 458.6 jit_solution(12702945503331707144)
XLA Ops:
  8.0 1.1 convolution_bitcast_fusion.6
  9.8 0.8 copy.82
  10.5 1.3 fusion.105
  12.5 1.2 dynamic_slice.24.refs_0_.len_ref
  14.4 157.7 %forward.1 = (bf16[4,4,48,3072]{3,2,1,0:T(8,128)(2,1)}, bf16[4,4,192,768]{3,2,1,0:T(8,128)(2,1)}, bf16[4,4,48,3072]{3,2,1,0:T(8,128)(2,1)}, bf16[4,4,192,768]{3,...) custom-call(s32[1]{0:T(128)} %dynamic_slice.24.refs_0_.len_ref, ...), custom_call_target="tpu_custom_call" | custom-call | tf_op jit(solution)/shard_map/forward/pallas_call | solution.py:600
  172.1 0.8 constant_dynamic-update-slice_fusion.17
  172.9 1.6 convolution_reduce_fusion.7
  174.5 1.6 convolution_reduce_fusion.6
  178.5 1.6 fusion.130
  182.3 3.2 fusion.100
  186.0 1.3 fusion.98
  187.4 0.7 convolution_reduce_fusion
  188.2 1.9 fusion.123
  192.1 1.1 multiply_reduce_fusion.13
  194.5 0.7 pad_bitcast_fusion
  196.5 0.8 fusion.131
  197.8 1.1 multiply_reduce_fusion
  200.4 8.6 %fusion.6 = bf16[512,3072]{1,0:T(8,128)(2,1)S(1)} fusion(f32[512,3072]{1,0:T(8,128)S(1)} %bitcast.234, bf16[3072,768]{1,0:T(8,128)(2,1)} %bitcast.240, f32[512,768]{1,0:T(8,128)S(1)} %get-tuple-element.198), kind=kOutput, calls=%fused_computation.8 | convolution fusion | flops 2447769600 | bytes 15728640 | tf_op jit(solution)/shard_map/dot_general | solution.py:48
  209.0 2.8 multiply_reduce_fusion.1
  212.6 0.9 copy-done.48
  213.4 0.8 convolution_convert_fusion.8.do_ref
  215.0 33.1 %attend_bwd.1 = (bf16[512,768]{1,0:T(8,128)(2,1)S(1)}, bf16[512,768]{1,0:T(8,128)(2,1)S(1)}, bf16[512,768]{1,0:T(8,128)(2,1)S(1)}, f32[12,1,1024]{2,1,0:T(1,128)S(1)}) custom-call(s32[1]{0:T(128)} %dynamic_slice.24.refs_0_.len_ref, f32[12,1,1024]{2,1,0:T(1,128)S(1)} %copy-done.3, bf16[512,768]{1,0:T(8,128)(2,1)S(1)} %copy-done, ...), custom_call_target="tpu_custom_call" | custom-call | tf_op jit(solution)/shard_map/attend_bwd/pallas_call | solution.py:196
  248.1 0.8 fusion.133
  249.4 0.8 fusion.132
  250.7 1.1 fusion.17
  251.9 1.5 fusion.13
  253.4 1.8 convolution_convert_fusion.5
  255.2 1.9 convolution_convert_fusion.6
  257.1 1.8 convolution_convert_fusion.7
  258.9 3.1 convolution_convert_fusion.4
  262.0 1.1 constant_dynamic-update-slice_fusion.5
  263.7 0.7 reshape.474
  265.0 0.7 copy-done.24
  265.7 1.1 constant_dynamic-update-slice_fusion.4
  266.8 1.1 constant_dynamic-update-slice_fusion.3
  268.5 1.1 constant_dynamic-update-slice_fusion.2
  269.6 0.8 convolution_convert_fusion.3
  270.4 1.1 constant_dynamic-update-slice_fusion.1
  271.9 0.8 convolution_convert_fusion.2
  272.7 1.1 constant_dynamic-update-slice_fusion.sq_ref
  273.8 4.5 convolution_convert_fusion.1
  278.3 5.3 %convolution_convert_fusion = bf16[3072,768]{1,0:T(8,128)(2,1)} fusion(f32[512,3072]{1,0:T(8,128)S(1)} %bitcast.236, f32[512,768]{1,0:T(8,128)S(1)} %copy-done.9), kind=kOutput, calls=%fused_computation.10 | convolution fusion | flops 2432827392 | bytes 12582912 | tf_op jit(solution)/shard_map/dot_general | solution.py:52
  283.6 115.8 %scatter_grads.1 = (f32[6,24,768]{2,1,0:T(8,128)}, f32[24,3072]{1,0:T(8,128)}, f32[96,768]{1,0:T(8,128)}, bf16[4,128,768]{2,1,0:T(8,128)(2,1)}) custom-call(bf16[6,4,4,48,768]{4,3,2,1,0:T(8,128)(2,1)} %constant_dynamic-update-slice_fusion.sq_ref, bf16[1,4,4,48,3072]{4,3,2,1,0:T(8,128)(2,1)} %bitcast.210, bf16[1,4,4,192,768]{4,3,2,1,0:T(8,128)(2,1)} %bitcast.211, ...), custom_call_target="tpu_custom_call" | custom-call | tf_op jit(solution)/shard_map/scatter_grads/pallas_call | solution.py:798
  399.4 2.5 convert_element_type.245
  402.6 1.6 constant_dynamic-slice_fusion.1
  404.3 3.2 copy.109
  407.5 0.9 constant_dynamic-slice_fusion
  408.8 1.5 copy.96
  410.2 1.4 copy.97
  411.6 0.8 copy.98
  412.4 0.8 fusion.23
  413.2 0.8 fusion.22
  414.2 0.9 slice_dynamic-update-slice_fusion.1
  415.1 0.8 copy.99
  416.1 0.8 multiply_reduce_fusion.6
  416.9 1.7 multiply_reduce_fusion.7
  418.6 0.7 multiply_reduce_fusion.8
  422.6 12.8 %total_all.1 = f32[8,896]{1,0:T(8,128)} custom-call(f32[8,896]{1,0:T(8,128)} %select_maximum_fusion.in_ref), custom_call_target="tpu_custom_call" | custom-call | tf_op jit(solution)/shard_map/total_all/pallas_call | solution.py:856
  435.3 1.4 fusion.129
  437.4 1.3 multiply_reduce_fusion.15
  442.1 2.7 multiply_subtract_fusion.1
  444.9 1.5 multiply_subtract_fusion.2
  447.1 1.8 multiply_subtract_fusion
  449.5 0.7 multiply_subtract_fusion.4
  (205 shorter events, 21.2 us)
Async XLA Ops:
  7.2 164.9 %copy-start.38 = (bf16[1,1,768]{2,1,0:T(2,128)(2,1)S(1)}, bf16[1,1,768]{2,1,0:T(2,128)(2,1)}, u32[]{:S(2)}) copy-start(bf16[1,1,768]{2,1,0:T(2,128)(2,1)} %param.21) | copy-start | bytes 4612
  7.2 395.4 %all-gather.3.cloned.1.call-start = ((), (), s32[]{:S(2)}) async-start(), calls=%async_computation | async-start | bytes 2703360 | tf_op jit(solution)/shard_map/all_gather | solution.py:1005
  172.1 6.1 %copy-start.12 = (bf16[4,4,48,768]{3,2,1,0:T(8,128)(2,1)S(1)}, bf16[4,4,48,768]{3,2,1,0:T(8,128)(2,1)}, u32[]{:S(2)}) copy-start(bf16[4,4,48,768]{3,2,1,0:T(8,128)(2,1)} %get-tuple-element.55) | copy-start | bytes 3538948
  172.1 6.1 %copy-start.31 = (f32[8,768]{1,0:T(8,128)S(1)}, f32[8,768]{1,0:T(8,128)}, u32[]{:S(2)}) copy-start(f32[8,768]{1,0:T(8,128)} %get-tuple-element.52) | copy-start | bytes 73732
  174.5 5.7 %copy-start.15 = (bf16[512,768]{1,0:T(8,128)(2,1)S(1)}, bf16[512,768]{1,0:T(8,128)(2,1)}, u32[]{:S(2)}) copy-start(bf16[512,768]{1,0:T(8,128)(2,1)} %get-tuple-element.57) | copy-start | bytes 2359300
  176.2 4.4 copy-start.14
  180.6 4.9 %copy-start.39 = (bf16[1,1,768]{2,1,0:T(2,128)(2,1)S(1)}, bf16[1,1,768]{2,1,0:T(2,128)(2,1)}, u32[]{:S(2)}) copy-start(bf16[1,1,768]{2,1,0:T(2,128)(2,1)} %param.22) | copy-start | bytes 4612
  182.3 3.8 copy-start.4
  182.3 5.9 %slice-start = ((s8[4718592]{0:T(1024)(128)(4,1)}), s8[4194304]{0:T(1024)(128)(4,1)S(1)}, s32[]{:S(2)}) async-start(s8[4718592]{0:T(1024)(128)(4,1)} %bitcast.198), calls=%async_computation.1 | async-start | bytes 8388608
  186.0 2.1 slice-start.1
  190.1 1.7 copy-start.30
  191.3 2.6 copy-start.13
  193.9 2.3 copy-start.5
  195.2 1.3 copy-start.49
  195.7 1.6 copy-start.16
  196.2 1.1 copy-start.28
  196.5 1.3 copy-start.27
  196.5 3.5 slice-start.2
  197.8 1.7 copy-start.7
  197.8 2.6 slice-start.3
  199.5 9.5 %slice-start.6 = ((s8[4718592]{0:T(1024)(128)(4,1)}), s8[4194304]{0:T(1024)(128)(4,1)S(1)}, s32[]{:S(2)}) async-start(s8[4718592]{0:T(1024)(128)(4,1)} %bitcast.237), calls=%async_computation.7 | async-start | bytes 8388608
  200.0 12.1 %copy-start.8 = (f32[512,768]{1,0:T(8,128)}, f32[512,768]{1,0:T(8,128)S(1)}, u32[]{:S(2)}) copy-start(f32[512,768]{1,0:T(8,128)S(1)} %get-tuple-element.198) | copy-start | bytes 4718596
  200.4 8.6 %slice-start.7 = ((s8[4718592]{0:T(1024)(128)(4,1)}), s8[524288]{0:T(1024)(128)(4,1)S(1)}, s32[]{:S(2)}) async-start(s8[4718592]{0:T(1024)(128)(4,1)} %bitcast.237), calls=%async_computation.8 | async-start | bytes 1048576
  209.0 2.9 copy-start.51
  209.0 2.9 copy-start.6
  212.2 1.3 copy-start.48
  213.4 1.1 copy-start
  213.4 1.4 copy-start.1
  213.4 1.6 copy-start.2
  213.4 1.6 copy-start.3
  215.0 33.1 %copy-start.47 = (bf16[4,4,48,768]{3,2,1,0:T(8,128)(2,1)S(1)}, bf16[4,4,48,768]{3,2,1,0:T(8,128)(2,1)}, u32[]{:S(2)}) copy-start(bf16[4,4,48,768]{3,2,1,0:T(8,128)(2,1)} %get-tuple-element.79) | copy-start | bytes 3538948
  248.1 1.3 copy-start.46
  249.4 1.3 copy-start.26
  258.9 3.1 copy-start.25
  262.0 2.4 copy-start.11
  264.4 1.3 copy-start.24
  264.4 2.4 copy-start.23
  266.8 1.7 copy-start.10
  267.9 1.7 copy-start.29
  267.9 1.7 copy-start.50
  270.4 1.5 copy-start.17
  271.9 1.9 copy-start.52
  272.7 5.6 %slice-start.4 = ((s8[6291456]{0:T(1024)(128)(4,1)}), s8[4194304]{0:T(1024)(128)(4,1)S(1)}, s32[]{:S(2)}) async-start(s8[6291456]{0:T(1024)(128)(4,1)} %bitcast.235), calls=%async_computation.5 | async-start | bytes 8388608
  273.8 4.5 copy-start.9
  273.8 4.5 slice-start.5
  399.4 3.1 copy-start.37
  407.5 11.1 %copy-start.21 = (f32[24,3072]{1,0:T(8,128)S(1)}, f32[24,3072]{1,0:T(8,128)}, u32[]{:S(2)}) copy-start(f32[24,3072]{1,0:T(8,128)} %get-tuple-element.84) | copy-start | bytes 884740
  408.8 33.3 %copy-start.19 = (f32[2,96,768]{2,1,0:T(8,128)S(1)}, f32[2,96,768]{2,1,0:T(8,128)}, u32[]{:S(2)}) copy-start(f32[2,96,768]{2,1,0:T(8,128)} %refs_4_.1) | copy-start | bytes 1769476
  416.1 26.0 %copy-start.22 = (f32[96,768]{1,0:T(8,128)S(1)}, f32[96,768]{1,0:T(8,128)}, u32[]{:S(2)}) copy-start(f32[96,768]{1,0:T(8,128)} %get-tuple-element.85) | copy-start | bytes 884740
  416.1 26.0 %copy-start.34 = (f32[2,96,768]{2,1,0:T(8,128)S(1)}, f32[2,96,768]{2,1,0:T(8,128)}, u32[]{:S(2)}) copy-start(f32[2,96,768]{2,1,0:T(8,128)} %param.32) | copy-start | bytes 1769476
  442.1 2.7 copy-start.20
  442.1 2.7 copy-start.35
  442.1 2.7 copy-start.36
  444.8 1.6 copy-start.18
  444.8 1.8 copy-start.32
  444.9 2.2 copy-start.33
  447.0 1.8 copy-start.41
  447.0 1.8 copy-start.42
  447.0 1.8 copy-start.43
  447.0 2.5 copy-start.40
  447.1 2.5 copy-start.44
  447.1 2.4 copy-start.45
Sparse Core Ops, SparseCore 0:
  195.3 57.5 all-gather.2
